TPU v7x, 128 devices: a whole 4x4x4 slice. The times are simulated.
128 devices in a mesh: leaf: 32 (over y, x, core), mp: 4 (over z).
Axes of the slice: x: 4, y: 4, z: 4, core: 2. Of those that a mesh axis runs over, the one named last changes fastest.
Arguments:
- tokens: bfloat16 [32768, 4608], P('leaf', 'mp'), may hold values from -6 to 6
- norm_gain: bfloat16 [4608], replicated, may hold values from 0.099609375 to 1.8984375
- w_query: bfloat16 [4608, 2048], P(None, 'mp'), may hold values from -0.25 to 0.25
- w_key: bfloat16 [4608, 1024], P(None, 'mp'), may hold values from -0.09375 to 0.09375
- w_value: bfloat16 [4608, 1024], P(None, 'mp'), may hold values from -0.09375 to 0.09375
- gen_node: int32 [512], P('leaf'), may hold values from 0 to 511, as said below
- partition: int32 [32], replicated, may hold values from 1 to 31, as said below
- parent: int32 [512], replicated, may hold values from 0 to 511, as said below
- block_mask: int32 [512, 512], replicated, may hold values from 0 to 1, as said below
Outputs:
- attended: bfloat16 [63488, 2048], P('leaf', 'mp')
Inputs may be any that keep to these rules, and one draw needn't show every extreme that they name: `gen_node`: A permutation of the nodes. At most 1 nodes of one device's generation slots belong to one subtree owner. `partition`: the counts sum to 512; owner d holds the consecutive nodes that start at the sum of the earlier counts. Node 0 is the root and its own parent; every other node's parent has a smaller number, and the numbers follow a depth-first order, so that a subtree's nodes are consecutive. block_mask[i, j] is 1 only where j is i or an ancestor of i; the diagonal is 1; a row holds at most 8 ones; at most 2 nodes of one owner are seen by nodes of other owners.
All inputs are finite; a program needn't handle non-finite values.
Results may differ from a plain program's by a relative error of at most 0.012.
The roundings to bfloat16 on the way count: a program that leaves them out, or rounds other values in their place, can miss the bound.
Values may be sent and summed in bfloat16 or wider, within the bound.
A program may use at most 128 MiB of HBM per device.

v0:
```python
import math

import jax
import jax.numpy as jnp
from jax import lax
from jax.sharding import PartitionSpec as P

HD = 128
CAP = 31
ANC = 8
EXPORT = 2


norm_epsilon = 1e-06
soft_cap = 50.0
query_scale = 144.0 ** (-0.5)
rope_base = 10000.0


def node_depth(parent):
    node_total = parent.shape[0]
    pointer = parent
    distance = (pointer != jnp.arange(node_total, dtype=jnp.int32)).astype(jnp.int32)
    for rounds in range(node_total.bit_length()):
        distance = distance + distance[pointer]
        pointer = pointer[pointer]
    return distance


def rotate_pairs(values, position):
    half_dim = values.shape[-1] // 2
    inverse_freq = jnp.exp(
        jnp.arange(half_dim, dtype=jnp.float32) * (-2.0 * math.log(rope_base) / values.shape[-1])
    )
    angles = position[..., None, None] * inverse_freq
    cosine = jnp.cos(angles)
    sine_part = jnp.sin(angles)
    first_half = values[..., :half_dim]
    second = values[..., half_dim:]
    return jnp.concatenate(
        [first_half * cosine - second * sine_part, second * cosine + first_half * sine_part],
        axis=-1,
    )


def select_blocks(visible, width):
    ranks = jnp.cumsum(visible, axis=1) - 1
    column = jnp.arange(visible.shape[1], dtype=jnp.int32)
    target = jnp.arange(width, dtype=jnp.int32)
    matched = visible[:, None, :] * (ranks[:, None, :] == target[None, :, None]).astype(jnp.int32)
    picked = jnp.sum(matched * column[None, None, :], axis=2)
    usable = jnp.sum(matched, axis=2)
    return (picked, usable)


def owner_of(node_ids, range_end):
    return jnp.sum((node_ids[:, None] >= range_end[None, :]).astype(jnp.int32), axis=1)


def make_fold(norm_gain, w_query, w_key, w_value):

    def accumulate(carried, shard_piece, offset):
        gain_part = norm_gain.astype(jnp.float32)
        wide = shard_piece.astype(jnp.float32)
        scaled = (wide * gain_part[None, :]).astype(jnp.bfloat16)
        query_acc = jnp.dot(scaled, w_query, preferred_element_type=jnp.float32)
        key_acc = jnp.dot(scaled, w_key, preferred_element_type=jnp.float32)
        value_acc = jnp.dot(scaled, w_value, preferred_element_type=jnp.float32)
        squares = jnp.sum(wide * wide, axis=1)
        return (query_acc, key_acc, value_acc, squares)

    return accumulate


def empty_carry(row_count, query_cols, key_cols):
    return (
        jnp.zeros((row_count, query_cols), jnp.float32),
        jnp.zeros((row_count, key_cols), jnp.float32),
        jnp.zeros((row_count, key_cols), jnp.float32),
        jnp.zeros((row_count,), jnp.float32),
    )


def finish(carried, node_ids, depth_all, node_tok, width):
    query_acc, key_acc, value_acc, squares = carried
    row_scale = lax.rsqrt(squares / width + norm_epsilon)[:, None]
    node_total = depth_all.shape[0]
    hit = node_ids[:, None] == jnp.arange(node_total, dtype=jnp.int32)[None, :]
    depth_of = jnp.sum(jnp.where(hit, depth_all[None, :], 0), axis=1)
    position = (
        depth_of[:, None] * node_tok + jnp.arange(node_tok, dtype=jnp.int32)[None, :]
    ).astype(jnp.float32)
    row_nodes = node_ids.shape[0]
    queries = rotate_pairs(
        (query_acc * row_scale).reshape(row_nodes, node_tok, -1, HD), position
    ).astype(jnp.bfloat16)
    key_rows = rotate_pairs(
        (key_acc * row_scale).reshape(row_nodes, node_tok, -1, HD), position
    ).astype(jnp.bfloat16)
    values = (value_acc * row_scale).astype(jnp.bfloat16)
    return (
        queries.reshape(row_nodes, -1),
        key_rows.reshape(row_nodes, -1),
        values.reshape(row_nodes, -1),
    )


def key_heads(flat_rows, node_tok, head_count):
    node_count = flat_rows.shape[0]
    return flat_rows.reshape(node_count, node_tok, head_count, HD).transpose(2, 0, 1, 3)


def attend_pool(queries, pool_key, pool_value, pool_ids, allowed, own_id, block_mask, node_tok):
    node_total = block_mask.shape[0]
    node_ids = jnp.arange(node_total, dtype=jnp.int32)
    own_rows = (own_id[:, None] == node_ids[None, :]).astype(jnp.int32)
    mask_rows = jnp.dot(own_rows, block_mask)
    pool_hit = ((pool_ids[:, None] == node_ids[None, :]) & allowed[:, None]).astype(jnp.int32)
    visible = (jnp.dot(mask_rows, pool_hit.T) > 0).astype(jnp.int32)
    picked, usable = select_blocks(visible, ANC)
    key_node = pool_ids[picked]
    head_count = pool_key.shape[0]
    query_len = queries.shape[2]
    key_len = ANC * node_tok
    query_tok = jnp.arange(query_len, dtype=jnp.int32) % node_tok
    key_tok = jnp.arange(key_len, dtype=jnp.int32) % node_tok
    causal = key_tok[None, :] <= query_tok[:, None]

    def one_slot(items):
        query_block, chosen, block_ids, block_use, self_id = items
        key_block = pool_key[:, chosen].reshape(head_count, key_len, HD)
        value_block = pool_value[:, chosen].reshape(head_count, key_len, HD)
        scores = (
            jnp.einsum("hqd,hkd->hqk", query_block, key_block, preferred_element_type=jnp.float32)
            * query_scale
        )
        capped = soft_cap * jnp.tanh(scores / soft_cap)
        column_ok = jnp.repeat(block_use > 0, node_tok)
        column_self = jnp.repeat(block_ids == self_id, node_tok)
        permitted = column_ok[None, :] & ((~column_self)[None, :] | causal)
        probs = jnp.where(permitted[None], jnp.exp(capped), 0.0)
        totals = jnp.sum(probs, axis=2)
        numer = jnp.einsum(
            "hqk,hkd->hqd",
            probs.astype(jnp.bfloat16),
            value_block,
            preferred_element_type=jnp.float32,
        )
        return (numer, totals)

    return lax.map(one_slot, (queries, picked, key_node, usable, own_id))


def on_device(tokens, norm_gain, w_query, w_key, w_value, gen_node, partition, parent, block_mask):
    leaf_count = lax.axis_size("leaf")
    leaf_index = lax.axis_index("leaf")
    node_total = parent.shape[0]
    node_dev = gen_node.shape[0]
    node_tok = tokens.shape[0] // node_dev
    feature_cols = tokens.shape[1]
    width = norm_gain.shape[0]
    query_cols = w_query.shape[1]
    key_cols = w_key.shape[1]
    head_count = key_cols // HD
    groups = query_cols // key_cols
    pair_cap = (CAP + leaf_count - 1) // leaf_count
    send_slots = leaf_count * pair_cap
    range_end = jnp.cumsum(partition)
    starts = range_end - partition
    my_start = starts[leaf_index]
    my_count = partition[leaf_index]
    slot_ids = jnp.arange(CAP, dtype=jnp.int32)
    own_id = jnp.where(slot_ids < my_count, my_start + slot_ids, -1)
    depth_all = node_depth(parent)
    owner_gen = owner_of(gen_node, range_end)
    local_ids = jnp.arange(node_dev, dtype=jnp.int32)
    earlier = jnp.sum(
        (
            (owner_gen[None, :] == owner_gen[:, None]) & (local_ids[None, :] < local_ids[:, None])
        ).astype(jnp.int32),
        axis=1,
    )
    target_slot = owner_gen * pair_cap + earlier
    send_map = target_slot[None, :] == jnp.arange(send_slots, dtype=jnp.int32)[:, None]
    send_ids = jnp.where(
        jnp.any(send_map, axis=1), jnp.sum(jnp.where(send_map, gen_node[None, :], 0), axis=1), -1
    )
    send_weights = send_map.astype(jnp.bfloat16)
    accumulate = make_fold(norm_gain, w_query, w_key, w_value)
    send_rows = jnp.dot(
        send_weights,
        tokens.reshape(node_dev, node_tok * feature_cols),
        preferred_element_type=jnp.float32,
    ).astype(jnp.bfloat16)
    recv_rows, recv_ids = (
        lax.all_to_all(send_rows, "leaf", split_axis=0, concat_axis=0, tiled=True),
        lax.all_to_all(send_ids, "leaf", split_axis=0, concat_axis=0, tiled=True),
    )
    take_map = ((own_id[:, None] == recv_ids[None, :]) & (own_id[:, None] >= 0)).astype(
        jnp.bfloat16
    )
    own_rows = jnp.dot(take_map, recv_rows, preferred_element_type=jnp.float32).astype(jnp.bfloat16)
    own_rows = own_rows.reshape(CAP * node_tok, feature_cols)
    carried = accumulate(
        empty_carry(CAP * node_tok, query_cols, key_cols),
        lax.all_gather(own_rows, "mp", axis=1, tiled=True),
        jnp.int32(0),
    )
    queries, key_rows, values = finish(carried, own_id, depth_all, node_tok, width)
    node_ids = jnp.arange(node_total, dtype=jnp.int32)
    owner_all = owner_of(node_ids, range_end)
    foreign = (owner_all[:, None] != owner_all[None, :]).astype(jnp.int32)
    seen_far = jnp.sum(block_mask * foreign, axis=0) > 0
    own_hit = own_id[:, None] == node_ids[None, :]
    seen_own = jnp.any(own_hit & seen_far[None, :], axis=1)
    export_rank = jnp.cumsum(seen_own.astype(jnp.int32)) - 1
    export_map = seen_own[None, :] & (
        export_rank[None, :] == jnp.arange(EXPORT, dtype=jnp.int32)[:, None]
    )
    export_ids = jnp.where(
        jnp.any(export_map, axis=1), jnp.sum(jnp.where(export_map, own_id[None, :], 0), axis=1), -1
    )
    export_weights = export_map.astype(jnp.bfloat16)
    export_keys = jnp.dot(export_weights, key_rows, preferred_element_type=jnp.float32).astype(
        jnp.bfloat16
    )
    export_values = jnp.dot(export_weights, values, preferred_element_type=jnp.float32).astype(
        jnp.bfloat16
    )
    own_allowed = own_id >= 0
    query_heads = (
        queries.reshape(CAP, node_tok, head_count, groups, HD)
        .transpose(0, 2, 3, 1, 4)
        .reshape(CAP, head_count, groups * node_tok, HD)
    )
    near_key = key_heads(key_rows, node_tok, head_count)
    near_value = key_heads(values, node_tok, head_count)
    far_keys, far_values, far_ids = (
        lax.all_gather(export_keys, "leaf", axis=0, tiled=True),
        lax.all_gather(export_values, "leaf", axis=0, tiled=True),
        lax.all_gather(export_ids, "leaf", axis=0, tiled=True),
    )
    far_allowed = (far_ids >= 0) & (owner_of(jnp.maximum(far_ids, 0), range_end) != leaf_index)
    pool_key = jnp.concatenate([near_key, key_heads(far_keys, node_tok, head_count)], axis=1)
    pool_value = jnp.concatenate([near_value, key_heads(far_values, node_tok, head_count)], axis=1)
    pool_ids = jnp.concatenate([own_id, far_ids], axis=0)
    pool_allowed = jnp.concatenate([own_allowed, far_allowed], axis=0)
    numer, totals = attend_pool(
        query_heads, pool_key, pool_value, pool_ids, pool_allowed, own_id, block_mask, node_tok
    )
    live = own_id >= 0
    safe_totals = jnp.where(live[:, None, None], totals, 1.0)
    result = jnp.where(live[:, None, None, None], numer / safe_totals[..., None], 0.0).astype(
        jnp.bfloat16
    )
    result = result.reshape(CAP, head_count, groups, node_tok, HD).transpose(0, 3, 1, 2, 4)
    return result.reshape(CAP * node_tok, query_cols)


def solution(mesh):
    in_specs = (
        P("leaf", "mp"),
        P(),
        P(None, "mp"),
        P(None, "mp"),
        P(None, "mp"),
        P("leaf"),
        P(),
        P(),
        P(),
    )
    out_specs = P("leaf", "mp")
    return jax.shard_map(
        on_device, mesh=mesh, in_specs=in_specs, out_specs=out_specs, check_vma=False
    )
```

profile of v0, /device:TPU:1, one launch (start us, length us, event | category | flops | bytes accessed | tf_op | source)
XLA Modules:
  0.0 739.1 jit_solution(7348886015908897405)
XLA Ops:
  10.2 8.6 %all-to-all-start = ((s32[32,1,1]{2,1,0:T(1,128)}), s32[32,1,1]{2,1,0:T(1,128)S(1)}, u32[]{:S(2)}, u32[]{:S(2)}) async-start(s32[32,1,1]{2,1,0:T(1,128)} %copy.78), calls=%async_computation | async-start | bytes 32768 | tf_op jit(solution)/shard_map/all_to_all | solution.py:197
  18.8 3.4 reshape.473
  22.1 5.3 fusion.14
  28.0 7.4 reduce.4
  35.4 7.0 reshape.684
  42.4 7.6 %all-to-all-start.1 = ((bf16[32,2,36864]{2,1,0:T(2,128)(2,1)}), bf16[32,2,36864]{2,1,0:T(2,128)(2,1)}, u32[]{:S(2)}, u32[]{:S(2)}) async-start(bf16[32,2,36864]{2,1,0:T(2,128)(2,1)} %reshape.684), calls=%async_computation.1 | async-start | bytes 9437184 | tf_op jit(solution)/shard_map/all_to_all | solution.py:196
  53.2 52.5 %all-to-all-done.1 = bf16[32,2,36864]{2,1,0:T(2,128)(2,1)} async-done(((bf16[32,2,36864]{2,1,0:T(2,128)(2,1)}), bf16[32,2,36864]{2,1,0:T(2,128)(2,1)}, u32[]{:S(2)}, u32[]{:S(2)}) %all-to-all-start.1) | async-done | bytes 4718624 | tf_op jit(solution)/shard_map/all_to_all | solution.py:196
  105.8 20.2 %reshape.685 = bf16[32,1,73728]{2,1,0:T(2,128)(2,1)} reshape(bf16[32,2,36864]{2,1,0:T(2,128)(2,1)} %all-to-all-done.1) | data formatting | bytes 9437184
  125.9 12.2 %convolution_convert_fusion = bf16[31,73728]{1,0:T(8,128)(2,1)} fusion(bf16[32,1,73728]{2,1,0:T(2,128)(2,1)} %reshape.685, s32[32]{0:T(128)S(1)} %reduce.2, s32[31]{0:T(128)S(1)} %get-tuple-element.335, pred[31]{0:T(512)(128)(4,1)S(1)} %get-tuple-element.199), kind=kOutput, calls=%fused_computation.46 | convolution fusion | flops 148563904 | bytes 9290011 | tf_op jit(solution)/shard_map/dot_general | solution.py:202
  138.1 7.1 reshape.474
  147.0 3.5 gather_fusion.4
  150.5 3.5 gather_fusion.3
  154.1 3.5 gather_fusion.6
  157.6 3.5 gather_fusion.5
  161.1 3.5 gather_fusion.8
  164.6 3.5 gather_fusion.7
  168.2 3.5 gather_fusion.10
  171.7 3.5 gather_fusion.9
  175.2 3.5 gather_fusion.12
  178.7 3.5 gather_fusion.11
  182.2 3.5 gather_fusion.14
  185.7 3.5 gather_fusion.13
  189.3 3.5 gather_fusion.16
  192.8 3.5 gather_fusion.15
  196.3 3.5 gather_fusion.18
  199.8 3.5 gather_fusion.17
  203.3 3.5 gather_fusion.20
  206.8 3.5 gather_fusion.19
  210.4 3.5 gather_fusion.21
  214.4 5.3 multiply_cosine_fusion
  219.7 94.6 %all-gather.6.cloned.1.call-done = bf16[1984,4608]{1,0:T(8,128)(2,1)} async-done(((bf16[1984,1152]{1,0:T(8,128)(2,1)}), bf16[1984,4608]{1,0:T(8,128)(2,1)}) %all-gather.6.cloned.1.call-update) | async-done | bytes 18284560 | tf_op jit(solution)/shard_map/all_gather | solution.py:206
  314.3 8.3 %fusion.16 = f32[1984]{0:T(1024)S(1)} fusion(bf16[1984,4608]{1,0:T(8,128)(2,1)} %all-gather.6.cloned.1.call-done), kind=kLoop, calls=%fused_computation.52 | loop fusion | flops 27424832 | bytes 18292480 | tf_op jit(solution)/shard_map/reduce_sum | solution.py:69
  322.6 12.7 %fusion.30 = f32[1984,256]{1,0:T(8,128)} fusion(bf16[4608,256]{1,0:T(8,128)(2,1)S(1)} %copy-done, bf16[1984,4608]{1,0:T(8,128)(2,1)} %all-gather.6.cloned.1.call-done, f32[4608]{0:T(1024)S(1)} %convert_element_type.99, f32[1984]{0:T(1024)S(1)} %add_rsqrt_fusion), kind=kOutput, calls=%fused_computation.68 | convolution fusion | flops 4708777984 | bytes 22701824 | tf_op jit(solution)/shard_map/dot_general | solution.py:67
  343.2 3.8 convert_element_type.104
  350.6 13.3 %all-reduce = s32[64]{0:T(128)S(1)} all-reduce(s32[64]{0:T(128)S(1)} %select_dynamic-update-slice_fusion), channel_id=1, replica_groups=mesh['leaf'=32,'mp'=4] {'leaf'}, use_global_device_ids=true, to_apply=%add | all-reduce | flops 64 | bytes 512
  367.6 13.1 %fusion.36 = bf16[1984,256]{1,0:T(8,128)(2,1)} fusion(bf16[4608,256]{1,0:T(8,128)(2,1)} %param.15, bf16[1984,4608]{1,0:T(8,128)(2,1)} %all-gather.6.cloned.1.call-done, f32[4608]{0:T(1024)S(1)} %convert_element_type.99, f32[1984]{0:T(1024)S(1)} %add_rsqrt_fusion), kind=kOutput, calls=%fused_computation.70 | convolution fusion | flops 4709285888 | bytes 21686016 | tf_op jit(solution)/shard_map/dot_general | solution.py:68
  380.7 2.5 reshape.479
  387.5 3.1 reshape_reshape.4
  390.6 16.2 %fusion.27 = f32[1984,512]{1,0:T(8,128)} fusion(bf16[4608,512]{1,0:T(8,128)(2,1)} %param.13, bf16[1984,4608]{1,0:T(8,128)(2,1)} %all-gather.6.cloned.1.call-done, f32[4608]{0:T(1024)S(1)} %convert_element_type.99, f32[1984]{0:T(1024)S(1)} %add_rsqrt_fusion), kind=kOutput, calls=%fused_computation.65 | convolution fusion | flops 9390129152 | bytes 27092736 | tf_op jit(solution)/shard_map/dot_general | solution.py:66
  406.8 5.3 reshape.475
  412.1 5.2 subtract_convert_fusion
  422.8 3.3 reshape.478
  428.1 10.4 %all-gather.10.cloned.1.call-done = bf16[32,2,16384]{2,1,0:T(2,128)(2,1)} async-done(((bf16[1,2,16384]{2,1,0:T(2,128)(2,1)}), bf16[32,2,16384]{2,1,0:T(2,128)(2,1)}) %all-gather.10.cloned.1.call-update) | async-done | bytes 2097168 | tf_op jit(solution)/shard_map/all_gather | solution.py:240
  438.4 3.6 reshape.480
  443.9 2.9 pad_maximum_fusion
  446.8 272.6 %while.16 = (s32[]{:T(128)}, f32[31,2,128,128]{3,2,1,0:T(8,128)}, f32[31,2,128]{2,1,0:T(2,128)S(1)}, s32[31,8]{1,0:T(8,128)S(1)}, s32[31,8]{1,0:T(8,128)S(1)}, /...) while((s32[]{:T(128)}, f32[31,2,128,128]{3,2,1,0:T(8,128)}, ...), condition=%wide.region_19.20_spmd.clone.clone, body=%wide.region_17.19_spmd.clone.sunk.clone | while | flops 67961648 | bytes 3487649 | solution.py:151
  446.8 2.5 gather_fusion
  449.3 2.5 gather_fusion.1
  455.6 2.5 gather_fusion
  458.1 2.5 gather_fusion.1
  464.4 2.5 gather_fusion
  466.9 2.5 gather_fusion.1
  473.2 2.5 gather_fusion
  475.7 2.5 gather_fusion.1
  482.0 2.5 gather_fusion
  484.5 2.5 gather_fusion.1
  537.2 2.5 gather_fusion.1
  569.9 2.5 gather_fusion
  578.7 2.5 gather_fusion
  640.3 2.5 gather_fusion
  713.2 2.5 gather_fusion.1
  719.5 3.6 select_convert_fusion
  723.2 3.4 copy.106
  726.6 5.7 reshape.482
  (616 shorter events, 271.6 us)
Async XLA Ops:
  6.5 316.1 %copy-start = (bf16[4608,256]{1,0:T(8,128)(2,1)S(1)}, bf16[4608,256]{1,0:T(8,128)(2,1)}, u32[]{:S(2)}) copy-start(bf16[4608,256]{1,0:T(8,128)(2,1)} %param.14) | copy-start | bytes 7077892
  10.2 32.2 %all-to-all-start = ((s32[32,1,1]{2,1,0:T(1,128)}), s32[32,1,1]{2,1,0:T(1,128)S(1)}, u32[]{:S(2)}, u32[]{:S(2)}) async-start(s32[32,1,1]{2,1,0:T(1,128)} %copy.78), calls=%async_computation | async-start | bytes 32768 | tf_op jit(solution)/shard_map/all_to_all | solution.py:197
  42.4 7.8 %copy-start.12 = (s32[32]{0:T(128)S(1)}, s32[32]{0:T(128)}, u32[]{:S(2)}) copy-start(s32[32]{0:T(128)} %param.17) | copy-start | bytes 388
  42.4 63.4 %all-to-all-start.1 = ((bf16[32,2,36864]{2,1,0:T(2,128)(2,1)}), bf16[32,2,36864]{2,1,0:T(2,128)(2,1)}, u32[]{:S(2)}, u32[]{:S(2)}) async-start(bf16[32,2,36864]{2,1,0:T(2,128)(2,1)} %reshape.684), calls=%async_computation.1 | async-start | bytes 9437184 | tf_op jit(solution)/shard_map/all_to_all | solution.py:196
  50.0 264.4 %all-gather.6.cloned.1.call-start = ((), (), s32[]{:S(2)}) async-start(), calls=%async_computation.2 | async-start | bytes 22855680 | tf_op jit(solution)/shard_map/all_gather | solution.py:206
  145.2 1.2 copy-start.8
  145.2 1.8 copy-start.11
  145.2 1.8 copy-start.2
  145.2 277.6 %all-gather.8.cloned.1.call-start = ((), (), s32[]{:S(2)}) async-start(), calls=%async_computation.3 | async-start | bytes 2162688 | tf_op jit(solution)/shard_map/all_gather | solution.py:239
  337.6 2.3 copy-start.3
  340.6 6.4 copy-start.5
  341.2 8.1 %copy-start.13 = (u32[128]{0:T(128)S(1)}, u32[128]{0:T(128)}, u32[]{:S(2)}) copy-start(u32[128]{0:T(128)} %constant.128) | copy-start | bytes 1540
  349.1 89.4 %all-gather.10.cloned.1.call-start = ((), (), s32[]{:S(2)}) async-start(), calls=%async_computation.4 | async-start | bytes 2162688 | tf_op jit(solution)/shard_map/all_gather | solution.py:240
  406.8 5.3 copy-start.4
  417.3 1.2 copy-start.10
  417.9 1.9 copy-start.6
  442.0 1.6 copy-start.7
  442.0 1.8 copy-start.9
  723.2 9.1 %copy-start.1 = (bf16[4608,256]{1,0:T(8,128)(2,1)S(1)}, bf16[4608,256]{1,0:T(8,128)(2,1)}, u32[]{:S(2)}) copy-start(bf16[4608,256]{1,0:T(8,128)(2,1)} %param.14) | copy-start | bytes 7077892
Sparse Core Ops, SparseCore 0:
  145.3 168.9 all-gather.5
  349.2 43.9 all-gather.7
  395.4 42.9 all-gather.9
where the time goes:
time: 750 us; the launch traced here: 739 us
  local copies, waits for them, and re-layouts  338 us (45%)
  waiting for transfers between devices  158 us (21%)
  matrix products  132 us (18%)
  other arithmetic  66 us (9%)
  starting transfers between devices  16.7 us (2%)
  between operations  14.8 us (2%)
  blocking collectives  13.3 us (2%)
    all_gather x1, waiting for transfers between devices, on_device(): lax.all_gather(own_rows, 'mp', axis=1, tiled=True)  94.6 us
    gather x62, local copies, waits for them, and re-layouts, one_slot(): value_block = pool_value[:, chosen].reshape(head_count, key_len, HD)  77.4 us
    gather x62, local copies, waits for them, and re-layouts, one_slot(): key_block = pool_key[:, chosen].reshape(head_count, key_len, HD)  77.4 us
    all_to_all x1, waiting for transfers between devices, on_device(): lax.all_to_all(send_rows, 'leaf', split_axis=0, concat_axis=0, tiled=True)  52.5 us
    dot_general x31, matrix products, one_slot(): jnp.einsum('hqd,hkd->hqk', query_block, key_block, preferred_element_type...  38.7 us
    gather x10, local copies, waits for them, and re-layouts, node_depth(): distance = distance + distance[pointer]  34.9 us
    gather x9, local copies, waits for them, and re-layouts, node_depth(): pointer = pointer[pointer]  31.4 us
    unnamed x32, local copies, waits for them, and re-layouts  30 us
  transfers between devices with their start and end apart: 5, of which 3 were waited for; matrix products, arithmetic and copies ran while one was open for 22% of the time, Pallas kernels for 0%

commit v1 on v0

v1 whole, which is shorter than its diff:
```python
import functools
import math

import jax
import jax.numpy as jnp
from jax import lax
from jax.experimental import pallas as pl
from jax.experimental.pallas import tpu as pltpu
from jax.sharding import PartitionSpec as P

HD = 128
CAP = 31
ANC = 8
EXPORT = 2
CHUNKS = 4
NODE_TOK = 64
TOK = NODE_TOK // CHUNKS

norm_epsilon = 1e-06
soft_cap = 50.0
query_scale = 144.0 ** (-0.5)
rope_base = 10000.0

MESH = pl.DeviceIdType.MESH


def project_kernel(
    leafs, nodes, width, q_cols, k_cols,
    gen_ref, part_ref, parent_ref, mask_ref, gain_ref, freq_ref, tok_ref, wq_ref, wk_ref, wv_ref,
    qkv_ref, far_ref, table_ref,
    pieces, weights, scaled, acc, squares, angle_cos, angle_sin, made, send, recv, far,
    ids_out, ids_in, export_src,
    depth_sm, index_sm, start_sm, end_sm,
    load_sem, own_sem, full_send, full_recv, half_send, half_recv, ids_send, ids_recv,
    slot_send, slot_recv, slot_own, qkv_sem, far_sem,
    x_send, x_recv, y_send, y_recv, core_send, core_recv,
):
    me = lax.axis_index("leaf")
    z = lax.axis_index("mp")
    mp = 4
    right, left = lax.rem(z + 1, mp), lax.rem(z + 3, mp)
    opposite = lax.rem(z + 2, mp)
    feat = width // mp
    rows = nodes * TOK
    cols = q_cols + 2 * k_cols
    half = nodes // 2
    node_total = parent_ref.shape[0]
    core = lax.rem(me, 2)
    chip = lax.div(me, 2)
    cx = lax.rem(chip, 4)
    cy = lax.div(chip, 4)

    loads = [
        pltpu.make_async_copy(wq_ref, weights.at[:, :, pl.ds(0, q_cols)], load_sem.at[0]),
        pltpu.make_async_copy(wk_ref, weights.at[:, :, pl.ds(q_cols, k_cols)], load_sem.at[1]),
        pltpu.make_async_copy(wv_ref, weights.at[:, :, pl.ds(q_cols + k_cols, k_cols)], load_sem.at[2]),
    ]

    def own_load(c):
        return pltpu.make_async_copy(
            tok_ref.at[:, pl.ds(pl.multiple_of(c * TOK, TOK), TOK), :], pieces.at[z, c], own_sem.at[c]
        )

    barrier = pltpu.get_barrier_semaphore()

    def greet(o, carry):
        peer = lax.rem(me + o, leafs)
        pl.semaphore_signal(barrier, inc=1, device_id=(peer, z), device_id_type=MESH)
        return carry

    lax.fori_loop(1, leafs, greet, 0)
    pl.semaphore_signal(barrier, inc=1, device_id=(me, right), device_id_type=MESH)
    pl.semaphore_signal(barrier, inc=1, device_id=(me, left), device_id_type=MESH)
    for c in range(CHUNKS):
        own_load(c).start()
    for load in loads:
        load.start()
    pl.semaphore_wait(barrier, leafs + 1)

    def full(side, c):
        return pltpu.make_async_remote_copy(
            src_ref=pieces.at[z, c],
            dst_ref=pieces.at[z, c],
            send_sem=full_send.at[side, c],
            recv_sem=full_recv.at[side, c],
            device_id=(me, right if side == 0 else left),
            device_id_type=MESH,
        )

    def full_arrival(side, c):
        source = left if side == 0 else right
        return pltpu.make_async_remote_copy(
            src_ref=pieces.at[source, c],
            dst_ref=pieces.at[source, c],
            send_sem=full_send.at[side, c],
            recv_sem=full_recv.at[side, c],
            device_id=(me, right if side == 0 else left),
            device_id_type=MESH,
        )

    def forward(side, c):
        source = left if side == 0 else right
        part = pieces.at[source, c, pl.ds(side * half, half)]
        return pltpu.make_async_remote_copy(
            src_ref=part,
            dst_ref=part,
            send_sem=half_send.at[side, c],
            recv_sem=half_recv.at[side, c],
            device_id=(me, right if side == 0 else left),
            device_id_type=MESH,
        )

    def forward_arrival(side, c):
        part = pieces.at[opposite, c, pl.ds(side * half, half)]
        return pltpu.make_async_remote_copy(
            src_ref=part,
            dst_ref=part,
            send_sem=half_send.at[side, c],
            recv_sem=half_recv.at[side, c],
            device_id=(me, right if side == 0 else left),
            device_id_type=MESH,
        )

    for c in range(2):
        own_load(c).wait()
        full(0, c).start()
        full(1, c).start()
    for c in range(2, CHUNKS):
        own_load(c).wait()

    def ranges(d, first):
        last = first + part_ref[d]
        start_sm[d] = first
        end_sm[d] = last
        found = jnp.int32(0)
        for b in range(nodes):
            node = gen_ref[b]
            found = found + jnp.where((node >= first) & (node < last), b + 1, 0)
        index_sm[d] = jnp.maximum(found - 1, 0)
        ids_out[d] = jnp.full((8, 128), jnp.where(found > 0, gen_ref[jnp.maximum(found - 1, 0)], -1), jnp.int32)
        return last

    lax.fori_loop(0, leafs, ranges, jnp.int32(0))

    def ids_copy(o):
        peer = lax.rem(me + o, leafs)
        return pltpu.make_async_remote_copy(
            src_ref=ids_out.at[peer],
            dst_ref=ids_in.at[me],
            send_sem=ids_send,
            recv_sem=ids_recv,
            device_id=(peer, z),
            device_id_type=MESH,
        )

    lax.fori_loop(1, leafs, lambda o, carry: (ids_copy(o).start(), carry)[1], 0)
    ids_in[me] = ids_out[me]

    depth_sm[0] = jnp.int32(0)

    def deeper(n, carry):
        depth_sm[n] = depth_sm[parent_ref[n]] + 1
        return carry

    lax.fori_loop(1, node_total, deeper, 0)

    token_row = lax.broadcasted_iota(jnp.int32, (TOK, HD), 0)
    sign = jnp.where(lax.broadcasted_iota(jnp.int32, (rows, HD), 1) < HD // 2, -1.0, 1.0)

    def tables(c, carry):
        def one_node(b, carry2):
            position = depth_sm[gen_ref[b]] * NODE_TOK + c * TOK + token_row
            at = pl.ds(pl.multiple_of(b * TOK, TOK), TOK)
            angle_cos[c, at, :] = position.astype(jnp.float32) * freq_ref[...]
            return carry2

        lax.fori_loop(0, nodes, one_node, 0)
        angles = angle_cos[c]
        angle_sin[c] = jnp.sin(angles) * sign
        angle_cos[c] = jnp.cos(angles)
        return carry

    lax.fori_loop(0, CHUNKS, tables, 0)

    lane8 = lax.broadcasted_iota(jnp.int32, (8, node_total), 1)

    def spans(step, carry):
        d = leafs - 1 - step
        end_of, start_of, owner = carry
        inside = lane8 < end_sm[d]
        return (
            jnp.where(inside, end_sm[d], end_of),
            jnp.where(inside, start_sm[d], start_of),
            jnp.where(inside, d, owner),
        )

    blank = jnp.zeros((8, node_total), jnp.int32)
    end_of, start_of, owner = lax.fori_loop(0, leafs, spans, (blank, blank, blank))
    my_start = start_sm[me]
    row_id = lax.broadcasted_iota(jnp.int32, (node_total, node_total), 0)
    col_id = lax.broadcasted_iota(jnp.int32, (node_total, node_total), 1)
    mask = mask_ref[...]
    foreign = (mask > 0) & (row_id >= end_of[0:1, :])
    seen = jnp.max(jnp.where(foreign, 1.0, 0.0), axis=0, keepdims=True)
    earlier = jnp.where((row_id < col_id) & (row_id >= start_of[0:1, :]), 1.0, 0.0).astype(jnp.bfloat16)
    seen8 = jnp.broadcast_to(seen, (8, node_total))
    rank8 = jnp.dot(seen8.astype(jnp.bfloat16), earlier, preferred_element_type=jnp.float32)
    owner_f = owner.astype(jnp.float32)
    core_f = lax.rem(owner, 2).astype(jnp.float32)
    chip_f = lax.div(owner, 2).astype(jnp.float32)
    far_place = leafs + core_f * leafs + chip_f * EXPORT + jnp.minimum(rank8, EXPORT - 1.0)
    relative = (lane8 - my_start).astype(jnp.float32)
    place = jnp.where(lane8 >= my_start, relative, far_place)

    slot_row = lax.broadcasted_iota(jnp.int32, (32, node_total), 0)
    slot_col = lax.broadcasted_iota(jnp.int32, (32, node_total), 1)
    own_here = slot_col == my_start + slot_row
    own_mask = jnp.dot(
        jnp.where(own_here, 1.0, 0.0).astype(jnp.bfloat16),
        jnp.where(mask > 0, 1.0, 0.0).astype(jnp.bfloat16),
        preferred_element_type=jnp.float32,
    )
    others = jnp.where((own_mask > 0.5) & ~own_here, 1.0, 0.0)
    before = jnp.where(row_id < col_id, 1.0, 0.0).astype(jnp.bfloat16)
    rank = jnp.dot(others.astype(jnp.bfloat16), before, preferred_element_type=jnp.float32)
    lane32 = lax.broadcasted_iota(jnp.int32, (32, 128), 1)
    row32 = lax.broadcasted_iota(jnp.int32, (32, 128), 0)
    table = jnp.zeros((32, 128), jnp.float32)
    for r in range(ANC - 1):
        hit = (others > 0.5) & (jnp.abs(rank - float(r)) < 0.5)
        value = jnp.sum(jnp.where(hit, place[0:1, :], 0.0), axis=1, keepdims=True)
        table = jnp.where(lane32 == r, value, table)
    table = jnp.where(lane32 == ANC - 1, jnp.sum(others, axis=1, keepdims=True), table)

    pltpu.make_async_copy(ids_in.at[pl.ds(0, leafs - 1)], ids_in.at[pl.ds(0, leafs - 1)], ids_recv).wait()

    def sources(s, total):
        return total + jnp.where(ids_in[s][0:1, :] == my_start + row32, s.astype(jnp.float32), 0.0)

    source = lax.fori_loop(0, leafs, sources, jnp.zeros((32, 128), jnp.float32))
    table = jnp.where(lane32 == 2 * ANC, source, table)
    table_ref[...] = table.astype(jnp.int32)
    mine8 = (lane8 >= my_start) & (owner == me) & (seen8 > 0.5)
    for k in range(EXPORT):
        picked = jnp.sum(
            jnp.where(mine8 & (jnp.abs(rank8 - float(k)) < 0.5), relative, 0.0), axis=1, keepdims=True
        )
        chosen = jnp.sum(
            jnp.where(row32.astype(jnp.float32) == picked[0:1, :], source, 0.0), axis=0, keepdims=True
        )
        export_src[k] = jnp.broadcast_to(chosen, (TOK, 128))

    for load in loads:
        load.wait()
    full_arrival(0, 0).wait_recv()
    forward(0, 0).start()
    full_arrival(1, 0).wait_recv()
    forward(1, 0).start()
    full(0, 2).start()
    full(1, 2).start()

    def accumulate(src, c, first):
        wide = pieces[src, c].reshape(rows, feat).astype(jnp.float32)
        gain = gain_ref[src]
        scaled[...] = (wide * gain).astype(jnp.bfloat16)
        part = jnp.sum(wide * wide, axis=1, keepdims=True)
        if first:
            squares[...] = jnp.broadcast_to(part, (rows, 128))
        else:
            squares[...] += jnp.broadcast_to(part, (rows, 128))
        product = jnp.dot(scaled[...], weights[src], preferred_element_type=jnp.float32)
        if first:
            acc[...] = product
        else:
            acc[...] += product

    def slot_copy(o, c):
        peer = lax.rem(me + o, leafs)
        return pltpu.make_async_remote_copy(
            src_ref=send.at[c, peer],
            dst_ref=recv.at[c, me],
            send_sem=slot_send.at[c],
            recv_sem=slot_recv.at[c],
            device_id=(peer, z),
            device_id_type=MESH,
        )

    def slots_arrived(c):
        part = recv.at[c, pl.ds(0, leafs - 1)]
        pltpu.make_async_copy(part, part, slot_recv.at[c]).wait()

    def qkv_out(c):
        return pltpu.make_async_copy(
            recv.at[c], qkv_ref.at[:, pl.ds(pl.multiple_of(c * TOK, TOK), TOK), :], qkv_sem.at[c]
        )

    def far_out(c):
        return pltpu.make_async_copy(
            far.at[c], far_ref.at[:, pl.ds(pl.multiple_of(c * TOK, TOK), TOK), :], far_sem.at[c]
        )

    block = ((core * 4 + cy) * 4 + cx) * EXPORT

    def x_copy(o, c):
        part = far.at[c, pl.ds(block, EXPORT)]
        peer = (cy * 4 + lax.rem(cx + o, 4)) * 2 + core
        return pltpu.make_async_remote_copy(
            src_ref=part, dst_ref=part, send_sem=x_send.at[o - 1, c], recv_sem=x_recv.at[o - 1, c],
            device_id=(peer, z), device_id_type=MESH,
        )

    def x_arrival(o, c):
        part = far.at[c, pl.ds(((core * 4 + cy) * 4 + lax.rem(cx + 4 - o, 4)) * EXPORT, EXPORT)]
        return pltpu.make_async_remote_copy(
            src_ref=part, dst_ref=part, send_sem=x_send.at[o - 1, c], recv_sem=x_recv.at[o - 1, c],
            device_id=(me, right), device_id_type=MESH,
        )

    def y_copy(o, c):
        part = far.at[c, pl.ds((core * 4 + cy) * 4 * EXPORT, 4 * EXPORT)]
        peer = (lax.rem(cy + o, 4) * 4 + cx) * 2 + core
        return pltpu.make_async_remote_copy(
            src_ref=part, dst_ref=part, send_sem=y_send.at[o - 1, c], recv_sem=y_recv.at[o - 1, c],
            device_id=(peer, z), device_id_type=MESH,
        )

    def y_arrival(o, c):
        part = far.at[c, pl.ds((core * 4 + lax.rem(cy + 4 - o, 4)) * 4 * EXPORT, 4 * EXPORT)]
        return pltpu.make_async_remote_copy(
            src_ref=part, dst_ref=part, send_sem=y_send.at[o - 1, c], recv_sem=y_recv.at[o - 1, c],
            device_id=(me, right), device_id_type=MESH,
        )

    def core_copy(c):
        part = far.at[c, pl.ds(core * 16 * EXPORT, 16 * EXPORT)]
        return pltpu.make_async_remote_copy(
            src_ref=part, dst_ref=part, send_sem=core_send.at[c], recv_sem=core_recv.at[c],
            device_id=(chip * 2 + 1 - core, z), device_id_type=MESH,
        )

    def core_arrival(c):
        part = far.at[c, pl.ds((1 - core) * 16 * EXPORT, 16 * EXPORT)]
        return pltpu.make_async_remote_copy(
            src_ref=part, dst_ref=part, send_sem=core_send.at[c], recv_sem=core_recv.at[c],
            device_id=(chip * 2 + 1 - core, z), device_id_type=MESH,
        )

    def export_x(c):
        slots_arrived(c)
        qkv_out(c).start()
        for k in range(EXPORT):
            for t in range(2 * k_cols // 128):
                lanes = pl.ds(q_cols + t * 128, 128)

                def pick(s, total):
                    return jnp.where(
                        export_src[k] == s.astype(jnp.float32), recv[c, s, :, lanes].astype(jnp.float32), total
                    )

                chosen = lax.fori_loop(0, leafs, pick, jnp.zeros((TOK, 128), jnp.float32))
                far[c, block + k, :, pl.ds(t * 128, 128)] = chosen.astype(jnp.bfloat16)
        for o in (1, 2, 3):
            x_copy(o, c).start()

    def export_y(c):
        for o in (1, 2, 3):
            x_arrival(o, c).wait_recv()
        for o in (1, 2, 3):
            y_copy(o, c).start()

    def export_core(c):
        for o in (1, 2, 3):
            y_arrival(o, c).wait_recv()
        core_copy(c).start()

    def one_chunk(c, carry):
        accumulate(z, c, True)
        accumulate(left, c, False)
        accumulate(right, c, False)

        @pl.when(c + 1 < CHUNKS)
        def _():
            full_arrival(0, c + 1).wait_recv()
            forward(0, c + 1).start()
            full_arrival(1, c + 1).wait_recv()
            forward(1, c + 1).start()

        @pl.when(c + 3 < CHUNKS)
        def _():
            full(0, c + 3).start()
            full(1, c + 3).start()

        @pl.when(c >= 2)
        def _():
            export_y(c - 2)

        forward_arrival(0, c).wait_recv()
        forward_arrival(1, c).wait_recv()
        accumulate(opposite, c, False)

        scale = lax.rsqrt(squares[...] / width + norm_epsilon)
        cosine = angle_cos[c]
        sine = angle_sin[c]
        for head in range(cols // HD):
            at = pl.ds(head * HD, HD)
            value = acc[:, at] * scale
            if head * HD < q_cols + k_cols:
                value = value * cosine + pltpu.roll(value, HD // 2, 1) * sine
            made[:, :, at] = value.astype(jnp.bfloat16).reshape(nodes, TOK, HD)

        def fill(d, carry2):
            send[c, d] = made[index_sm[d]]
            return carry2

        lax.fori_loop(0, leafs, fill, 0)
        lax.fori_loop(1, leafs, lambda o, carry2: (slot_copy(o, c).start(), carry2)[1], 0)
        recv[c, me] = send[c, me]

        @pl.when(c >= 2)
        def _():
            export_core(c - 2)

        @pl.when(c >= 1)
        def _():
            export_x(c - 1)

        return carry

    lax.fori_loop(0, CHUNKS, one_chunk, 0)

    last = CHUNKS - 1
    export_y(last - 1)
    export_x(last)
    export_core(last - 1)
    export_y(last)
    export_core(last)

    def settle(c, carry):
        core_arrival(c).wait_recv()
        far_out(c).start()
        for side in (0, 1):
            full(side, c).wait_send()
            forward(side, c).wait_send()
        sent = send.at[c, pl.ds(0, leafs - 1)]
        pltpu.make_async_copy(sent, sent, slot_send.at[c]).wait()
        for o in (1, 2, 3):
            x_copy(o, c).wait_send()
            y_copy(o, c).wait_send()
        core_copy(c).wait_send()
        qkv_out(c).wait()
        far_out(c).wait()
        return carry

    lax.fori_loop(0, CHUNKS, settle, 0)
    pltpu.make_async_copy(ids_out.at[pl.ds(0, leafs - 1)], ids_out.at[pl.ds(0, leafs - 1)], ids_send).wait()


def project(tokens, gain, freq, w_query, w_key, w_value, gen_node, partition, parent, block_mask, leafs):
    nodes = gen_node.shape[0]
    feat = tokens.shape[1]
    width = gain.shape[-1] * 4
    q_cols = w_query.shape[1]
    k_cols = w_key.shape[1]
    cols = q_cols + 2 * k_cols
    rows = nodes * TOK
    node_total = parent.shape[0]
    bf16, f32, i32 = jnp.bfloat16, jnp.float32, jnp.int32
    dma = pltpu.SemaphoreType.DMA
    smem = pl.BlockSpec(memory_space=pltpu.SMEM)
    vmem = pl.BlockSpec(memory_space=pltpu.VMEM)
    hbm = pl.BlockSpec(memory_space=pl.ANY)
    return pl.pallas_call(
        functools.partial(project_kernel, leafs, nodes, width, q_cols, k_cols),
        out_shape=(
            jax.ShapeDtypeStruct((leafs, NODE_TOK, cols), bf16),
            jax.ShapeDtypeStruct((leafs * EXPORT, NODE_TOK, 2 * k_cols), bf16),
            jax.ShapeDtypeStruct((32, 128), i32),
        ),
        in_specs=[smem, smem, smem, vmem, vmem, vmem, hbm, hbm, hbm, hbm],
        out_specs=(hbm, hbm, vmem),
        scratch_shapes=[
            pltpu.VMEM((4, CHUNKS, nodes, TOK, feat), bf16),
            pltpu.VMEM((4, feat, cols), bf16),
            pltpu.VMEM((rows, feat), bf16),
            pltpu.VMEM((rows, cols), f32),
            pltpu.VMEM((rows, 128), f32),
            pltpu.VMEM((CHUNKS, rows, HD), f32),
            pltpu.VMEM((CHUNKS, rows, HD), f32),
            pltpu.VMEM((nodes, TOK, cols), bf16),
            pltpu.VMEM((CHUNKS, leafs, TOK, cols), bf16),
            pltpu.VMEM((CHUNKS, leafs, TOK, cols), bf16),
            pltpu.VMEM((CHUNKS, leafs * EXPORT, TOK, 2 * k_cols), bf16),
            pltpu.VMEM((leafs, 8, 128), i32),
            pltpu.VMEM((leafs, 8, 128), i32),
            pltpu.VMEM((EXPORT, TOK, 128), f32),
            pltpu.SMEM((node_total,), i32),
            pltpu.SMEM((leafs,), i32),
            pltpu.SMEM((leafs,), i32),
            pltpu.SMEM((leafs,), i32),
            dma((3,)),
            dma((CHUNKS,)),
            dma((2, CHUNKS)),
            dma((2, CHUNKS)),
            dma((2, CHUNKS)),
            dma((2, CHUNKS)),
            dma,
            dma,
            dma((CHUNKS,)),
            dma((CHUNKS,)),
            dma((CHUNKS,)),
            dma((CHUNKS,)),
            dma((CHUNKS,)),
            dma((3, CHUNKS)),
            dma((3, CHUNKS)),
            dma((3, CHUNKS)),
            dma((3, CHUNKS)),
            dma((CHUNKS,)),
            dma((CHUNKS,)),
        ],
        compiler_params=pltpu.CompilerParams(
            collective_id=0, has_side_effects=True, vmem_limit_bytes=60 * 1024 * 1024
        ),
        cost_estimate=pl.CostEstimate(
            flops=2 * nodes * NODE_TOK * width * cols, bytes_accessed=30_000_000, transcendentals=0
        ),
        name="project_exchange",
    )(
        gen_node, partition, parent, block_mask, gain, freq,
        tokens.reshape(nodes, NODE_TOK, feat),
        w_query.reshape(4, feat, q_cols), w_key.reshape(4, feat, k_cols), w_value.reshape(4, feat, k_cols),
    )


def attend_kernel(
    q_cols, k_cols, table_ref, count_ref, qkv_ref, far_ref, out_ref, query, pool, load_sem
):
    leafs = qkv_ref.shape[0]
    loads = [
        pltpu.make_async_copy(qkv_ref.at[:, :, pl.ds(0, q_cols)], query, load_sem.at[0]),
        pltpu.make_async_copy(
            qkv_ref.at[:, :, pl.ds(q_cols, 2 * k_cols)], pool.at[pl.ds(0, leafs)], load_sem.at[1]
        ),
        pltpu.make_async_copy(far_ref, pool.at[pl.ds(leafs, far_ref.shape[0])], load_sem.at[2]),
    ]
    for load in loads:
        load.start()
    out_ref[...] = jnp.zeros_like(out_ref)
    for load in loads:
        load.wait()
    count = count_ref[0]
    heads = k_cols // HD
    groups = q_cols // k_cols
    q_rows = groups * NODE_TOK

    def attend(r, blocks, seen):
        own = table_ref[r, 2 * ANC]
        places = [own]
        for p in range(1, blocks):
            v = table_ref[r, p - 1]
            near = table_ref[jnp.minimum(v, leafs - 1), 2 * ANC]
            place = jnp.where(v < leafs, near, v)
            places.append(jnp.where(p < seen, place, own))
        width = blocks * NODE_TOK
        key_col = lax.broadcasted_iota(jnp.int32, (q_rows, width), 1)
        query_tok = lax.rem(lax.broadcasted_iota(jnp.int32, (q_rows, width), 0), NODE_TOK)
        allowed = ((key_col >= NODE_TOK) | (key_col <= query_tok)) & (key_col < seen * NODE_TOK)
        at = pl.ds(pl.multiple_of(r * NODE_TOK, NODE_TOK), NODE_TOK)
        for h in range(heads):
            keys = jnp.concatenate([pool[p, :, pl.ds(h * HD, HD)] for p in places], axis=0)
            values = jnp.concatenate([pool[p, :, pl.ds(k_cols + h * HD, HD)] for p in places], axis=0)
            queries = jnp.concatenate(
                [query[own, :, pl.ds((h * groups + g) * HD, HD)] for g in range(groups)], axis=0
            )
            scores = lax.dot_general(
                queries, keys, (((1,), (1,)), ((), ())), preferred_element_type=jnp.float32
            )
            capped = jnp.tanh(scores * (query_scale / soft_cap)) * soft_cap
            probs = jnp.where(allowed, jnp.exp(capped), 0.0)
            totals = jnp.sum(probs, axis=1, keepdims=True)
            numer = jnp.dot(probs.astype(jnp.bfloat16), values, preferred_element_type=jnp.float32)
            result = (numer / totals).astype(jnp.bfloat16)
            for g in range(groups):
                out_ref[at, pl.ds((h * groups + g) * HD, HD)] = result[g * NODE_TOK : (g + 1) * NODE_TOK]

    def one_node(r, carry):
        seen = table_ref[r, ANC - 1] + 1
        for low, high in ((0, 2), (2, 4), (4, 6), (6, 8)):

            @pl.when((seen > low) & (seen <= high))
            def _(high=high):
                attend(r, high, seen)

        return carry

    lax.fori_loop(0, count, one_node, 0)


def attend_all(table, count, qkv, far, q_cols, k_cols):
    bf16 = jnp.bfloat16
    leafs = qkv.shape[0]
    hbm = pl.BlockSpec(memory_space=pl.ANY)
    return pl.pallas_call(
        functools.partial(attend_kernel, q_cols, k_cols),
        out_shape=jax.ShapeDtypeStruct((CAP * NODE_TOK, q_cols), bf16),
        grid_spec=pltpu.PrefetchScalarGridSpec(
            num_scalar_prefetch=2,
            grid=(),
            in_specs=[hbm, hbm],
            out_specs=pl.BlockSpec(memory_space=pltpu.VMEM),
            scratch_shapes=[
                pltpu.VMEM((leafs, NODE_TOK, q_cols), bf16),
                pltpu.VMEM((leafs + far.shape[0], NODE_TOK, 2 * k_cols), bf16),
                pltpu.SemaphoreType.DMA((3,)),
            ],
        ),
        compiler_params=pltpu.CompilerParams(vmem_limit_bytes=40 * 1024 * 1024),
        name="attend",
    )(table, count, qkv, far)


def on_device(tokens, norm_gain, w_query, w_key, w_value, gen_node, partition, parent, block_mask):
    leafs = lax.axis_size("leaf")
    leaf_index = lax.axis_index("leaf")
    feat = tokens.shape[1]
    gain = norm_gain.astype(jnp.float32).reshape(-1, 1, feat)
    half_dim = HD // 2
    inverse_freq = jnp.exp(jnp.arange(half_dim, dtype=jnp.float32) * (-2.0 * math.log(rope_base) / HD))
    freq = jnp.concatenate([inverse_freq, inverse_freq])[None, :]
    qkv, far, table = project(
        tokens, gain, freq, w_query, w_key, w_value, gen_node, partition, parent, block_mask, leafs
    )
    count = lax.dynamic_slice(partition, (leaf_index,), (1,))
    return attend_all(table, count, qkv, far, w_query.shape[1], w_key.shape[1])


def solution(mesh):
    in_specs = (
        P("leaf", "mp"),
        P(),
        P(None, "mp"),
        P(None, "mp"),
        P(None, "mp"),
        P("leaf"),
        P(),
        P(),
        P(),
    )
    out_specs = P("leaf", "mp")
    return jax.shard_map(
        on_device, mesh=mesh, in_specs=in_specs, out_specs=out_specs, check_vma=False
    )
```

time: 750 us -> 168 us (0.22)
  the two profiles are of different devices: /device:TPU:1 before, /device:TPU:6 now
where the time goes in v1:
time: 168 us
  Pallas kernels  159 us (95%)
  local copies, waits for them, and re-layouts  7.72 us (5%)
    pallas_call x1, Pallas kernels, project(): pl.pallas_call(functools.partial(project_kernel, leafs, nodes, width, q_c...  140 us
    pallas_call x1, Pallas kernels, attend_all(): pl.pallas_call(functools.partial(attend_kernel, q_cols, k_cols), out_shap...  19.4 us
    unnamed x6, local copies, waits for them, and re-layouts  5.09 us

profile of v1, /device:TPU:6, one launch (start us, length us, event | category | flops | bytes accessed | tf_op | source)
XLA Modules:
  0.0 167.8 jit_solution(9386226397919073844)
XLA Ops:
  0.0 1.3 dynamic_slice.3.count_ref
  1.3 0.6 maximum_bitcast_fusion.freq_ref
  2.0 1.3 reshape.24.gain_ref
  3.3 140.0 %project_exchange.1 = (bf16[32,64,1024]{2,1,0:T(8,128)(2,1)}, bf16[64,64,512]{2,1,0:T(8,128)(2,1)}, s32[32,128]{1,0:T(8,128)}) custom-call(s32[16]{0:T(128)} %gen_ref.1, s32[32]{0:T(128)} %part_ref.1, s32[512]{0:T(512)} %parent_ref.1, s32[512,512]{1,0:T(8,128)} %mask_ref.1, f32[4,1,1152]{2,1,0:T(1,128)} %reshape.24.gain_ref, ...), custom_call_target="tpu_custom_call" | custom-call | flops 9663676416 | bytes 30000000 | tf_op jit(solution)/shard_map/project_exchange/pallas_call | solution.py:472
  143.3 0.0 copy-start
  143.3 2.2 %copy-done = bf16[32,64,1024]{2,1,0:T(8,128)(2,1)S(1)} copy-done((bf16[32,64,1024]{2,1,0:T(8,128)(2,1)S(1)}, bf16[32,64,1024]{2,1,0:T(8,128)(2,1)}, u32[]{:S(2)}) %copy-start) | copy-done | bytes 4194328
  145.5 0.0 copy-start.1
  145.5 2.2 %copy-done.1 = bf16[64,64,512]{2,1,0:T(8,128)(2,1)S(1)} copy-done((bf16[64,64,512]{2,1,0:T(8,128)(2,1)S(1)}, bf16[64,64,512]{2,1,0:T(8,128)(2,1)}, u32[]{:S(2)}) %copy-start.1) | copy-done | bytes 4194328
  147.7 0.0 copy-start.2
  147.7 0.7 copy-done.2
  148.4 19.4 %attend.1 = bf16[1984,512]{1,0:T(8,128)(2,1)} custom-call(s32[32,128]{1,0:T(8,128)S(1)} %copy-done.2, s32[1]{0:T(128)} %dynamic_slice.3.count_ref, bf16[32,64,1024]{2,1,0:T(8,128)(2,1)S(1)} %copy-done, bf16[64,64,512]{2,1,0:T(8,128)(2,1)S(1)} %copy-done.1), custom_call_target="tpu_custom_call" | custom-call | tf_op jit(solution)/shard_map/attend/pallas_call | solution.py:602
  (1 shorter events, 0.0 us)
Async XLA Ops:
  143.3 2.2 %copy-start = (bf16[32,64,1024]{2,1,0:T(8,128)(2,1)S(1)}, bf16[32,64,1024]{2,1,0:T(8,128)(2,1)}, u32[]{:S(2)}) copy-start(bf16[32,64,1024]{2,1,0:T(8,128)(2,1)} %get-tuple-element.9.qkv_ref) | copy-start | bytes 12582916
  145.5 2.2 %copy-start.1 = (bf16[64,64,512]{2,1,0:T(8,128)(2,1)S(1)}, bf16[64,64,512]{2,1,0:T(8,128)(2,1)}, u32[]{:S(2)}) copy-start(bf16[64,64,512]{2,1,0:T(8,128)(2,1)} %get-tuple-element.10.far_ref) | copy-start | bytes 12582916
  147.7 0.7 copy-start.2

commit v2 on v1

v2 whole, which is shorter than its diff:
```python
import functools
import math

import jax
import jax.numpy as jnp
import numpy as np
from jax import lax
from jax.experimental import pallas as pl
from jax.experimental.pallas import tpu as pltpu
from jax.sharding import PartitionSpec as P

HD = 128
CAP = 31
ANC = 8
EXPORT = 2
CHUNKS = 4
NODE_TOK = 64
TOK = NODE_TOK // CHUNKS
SLOTS = CAP
BATCH = 4

norm_epsilon = 1e-06
soft_cap = 50.0
query_scale = 144.0 ** (-0.5)
rope_base = 10000.0

MESH = pl.DeviceIdType.MESH


def fused_kernel(
    leafs, nodes, width, q_cols, k_cols,
    gen_ref, part_ref, parent_ref, mask_ref, gain_ref, freq_ref, tok_ref, wq_ref, wk_ref, wv_ref,
    out_ref,
    pieces, weights, scaled, acc, squares, angle_cos, angle_sin, made, send, recv, far,
    query, pool, numer, total, ids_out, ids_in, table_vm, gain_vm,
    depth_sm, index_sm, start_sm, end_sm, table_sm, place_sm,
    load_sem, own_sem, full_send, full_recv, half_send, half_recv, ids_send, ids_recv, table_sem,
    slot_send, slot_recv, chip_send, chip_recv, core_send, core_recv,
):
    me = lax.axis_index("leaf")
    z = lax.axis_index("mp")
    mp = 4
    right, left = lax.rem(z + 1, mp), lax.rem(z + 3, mp)
    opposite = lax.rem(z + 2, mp)
    feat = width // mp
    rows = nodes * TOK
    cols = q_cols + 2 * k_cols
    half = nodes // 2
    node_total = parent_ref.shape[0]
    core = lax.rem(me, 2)
    chip = lax.div(me, 2)
    chips = leafs // 2

    loads = [
        pltpu.make_async_copy(wq_ref, weights.at[:, :, pl.ds(0, q_cols)], load_sem.at[0]),
        pltpu.make_async_copy(wk_ref, weights.at[:, :, pl.ds(q_cols, k_cols)], load_sem.at[1]),
        pltpu.make_async_copy(wv_ref, weights.at[:, :, pl.ds(q_cols + k_cols, k_cols)], load_sem.at[2]),
    ]

    def own_load(c):
        return pltpu.make_async_copy(
            tok_ref.at[:, pl.ds(pl.multiple_of(c * TOK, TOK), TOK), :], pieces.at[z, c], own_sem.at[c]
        )

    barrier = pltpu.get_barrier_semaphore()

    def greet(o, carry):
        peer = lax.rem(me + o, leafs)
        pl.semaphore_signal(barrier, inc=1, device_id=(peer, z), device_id_type=MESH)
        return carry

    lax.fori_loop(1, leafs, greet, 0)
    pl.semaphore_signal(barrier, inc=1, device_id=(me, right), device_id_type=MESH)
    pl.semaphore_signal(barrier, inc=1, device_id=(me, left), device_id_type=MESH)
    for c in range(CHUNKS):
        own_load(c).start()
    for load in loads:
        load.start()
    pl.semaphore_wait(barrier, leafs + 1)

    def full(side, part, c):
        piece = pieces.at[z, c, pl.ds(part * half, half)]
        return pltpu.make_async_remote_copy(
            src_ref=piece,
            dst_ref=piece,
            send_sem=full_send.at[side, part, c],
            recv_sem=full_recv.at[side, part, c],
            device_id=(me, right if side == 0 else left),
            device_id_type=MESH,
        )

    def full_arrival(side, part, c):
        piece = pieces.at[left if side == 0 else right, c, pl.ds(part * half, half)]
        return pltpu.make_async_remote_copy(
            src_ref=piece,
            dst_ref=piece,
            send_sem=full_send.at[side, part, c],
            recv_sem=full_recv.at[side, part, c],
            device_id=(me, right if side == 0 else left),
            device_id_type=MESH,
        )

    def forward(side, c):
        source = left if side == 0 else right
        part = pieces.at[source, c, pl.ds(side * half, half)]
        return pltpu.make_async_remote_copy(
            src_ref=part,
            dst_ref=part,
            send_sem=half_send.at[side, c],
            recv_sem=half_recv.at[side, c],
            device_id=(me, right if side == 0 else left),
            device_id_type=MESH,
        )

    def forward_arrival(side, c):
        part = pieces.at[opposite, c, pl.ds(side * half, half)]
        return pltpu.make_async_remote_copy(
            src_ref=part,
            dst_ref=part,
            send_sem=half_send.at[side, c],
            recv_sem=half_recv.at[side, c],
            device_id=(me, right if side == 0 else left),
            device_id_type=MESH,
        )

    for c in range(CHUNKS):
        own_load(c).wait()
        if c == 0:
            for step in (0, 1):
                for side in (0, 1):
                    full(side, side ^ step, 0).start()

    def pass_on(c):
        for side in (0, 1):
            full_arrival(side, side, c).wait_recv()
            forward(side, c).start()

        @pl.when(c + 1 < CHUNKS)
        def _():
            for side in (0, 1):
                full(side, side, c + 1).start()

        for side in (0, 1):
            full_arrival(side, 1 - side, c).wait_recv()

        @pl.when(c + 1 < CHUNKS)
        def _():
            for side in (0, 1):
                full(side, 1 - side, c + 1).start()

    for part in range(mp):
        gain_vm[part] = gain_ref[pl.ds(part * feat, feat)].astype(jnp.float32).reshape(1, feat)

    def ranges(d, first):
        last = first + part_ref[d]
        start_sm[d] = first
        end_sm[d] = last
        found = jnp.int32(0)
        for b in range(nodes):
            node = gen_ref[b]
            found = found + jnp.where((node >= first) & (node < last), b + 1, 0)
        local = jnp.clip(found - 1, 0, nodes - 1)
        index_sm[d] = local
        ids_out[d] = jnp.full((8, 128), jnp.where(found > 0, gen_ref[local], -1), jnp.int32)
        return last

    lax.fori_loop(0, leafs, ranges, jnp.int32(0))

    def ids_copy(o):
        peer = lax.rem(me + o, leafs)
        return pltpu.make_async_remote_copy(
            src_ref=ids_out.at[peer],
            dst_ref=ids_in.at[me],
            send_sem=ids_send,
            recv_sem=ids_recv,
            device_id=(peer, z),
            device_id_type=MESH,
        )

    lax.fori_loop(1, leafs, lambda o, carry: (ids_copy(o).start(), carry)[1], 0)
    ids_in[me] = ids_out[me]

    depth_sm[0] = jnp.int32(0)

    def deeper(n, carry):
        depth_sm[n] = depth_sm[parent_ref[n]] + 1
        return carry

    lax.fori_loop(1, node_total, deeper, 0)

    pass_on(jnp.int32(0))

    token_row = lax.broadcasted_iota(jnp.int32, (TOK, HD), 0)
    sign = jnp.where(lax.broadcasted_iota(jnp.int32, (rows, HD), 1) < HD // 2, -1.0, 1.0)

    def tables(c, carry):
        def one_node(b, carry2):
            position = depth_sm[gen_ref[b]] * NODE_TOK + c * TOK + token_row
            at = pl.ds(pl.multiple_of(b * TOK, TOK), TOK)
            angle_cos[c, at, :] = position.astype(jnp.float32) * freq_ref[...]
            return carry2

        lax.fori_loop(0, nodes, one_node, 0)
        angles = angle_cos[c]
        angle_sin[c] = jnp.sin(angles) * sign
        angle_cos[c] = jnp.cos(angles)
        return carry

    lax.fori_loop(0, CHUNKS, tables, 0)

    lane8 = lax.broadcasted_iota(jnp.int32, (8, node_total), 1)

    def spans(step, carry):
        d = leafs - 1 - step
        end_of, start_of, owner = carry
        inside = lane8 < end_sm[d]
        return (
            jnp.where(inside, end_sm[d], end_of),
            jnp.where(inside, start_sm[d], start_of),
            jnp.where(inside, d, owner),
        )

    blank = jnp.zeros((8, node_total), jnp.int32)
    end_of, start_of, owner = lax.fori_loop(0, leafs, spans, (blank, blank, blank))
    my_start = start_sm[me]
    row_id = lax.broadcasted_iota(jnp.int32, (node_total, node_total), 0)
    col_id = lax.broadcasted_iota(jnp.int32, (node_total, node_total), 1)
    mask = mask_ref[...]
    foreign = (mask > 0) & (row_id >= end_of[0:1, :])
    seen = jnp.max(jnp.where(foreign, 1.0, 0.0), axis=0, keepdims=True)
    earlier = jnp.where((row_id < col_id) & (row_id >= start_of[0:1, :]), 1.0, 0.0).astype(jnp.bfloat16)
    seen8 = jnp.broadcast_to(seen, (8, node_total))
    rank8 = jnp.dot(seen8.astype(jnp.bfloat16), earlier, preferred_element_type=jnp.float32)
    owner_f = owner.astype(jnp.float32)
    core_f = lax.rem(owner, 2).astype(jnp.float32)
    chip_f = lax.div(owner, 2).astype(jnp.float32)
    far_place = leafs + core_f * leafs + chip_f * EXPORT + jnp.minimum(rank8, EXPORT - 1.0)
    relative = (lane8 - my_start).astype(jnp.float32)
    place = jnp.where(lane8 >= my_start, relative, far_place)

    slot_row = lax.broadcasted_iota(jnp.int32, (32, node_total), 0)
    slot_col = lax.broadcasted_iota(jnp.int32, (32, node_total), 1)
    own_here = slot_col == my_start + slot_row
    own_mask = jnp.dot(
        jnp.where(own_here, 1.0, 0.0).astype(jnp.bfloat16),
        jnp.where(mask > 0, 1.0, 0.0).astype(jnp.bfloat16),
        preferred_element_type=jnp.float32,
    )
    others = jnp.where((own_mask > 0.5) & ~own_here, 1.0, 0.0)
    before = jnp.where(row_id < col_id, 1.0, 0.0).astype(jnp.bfloat16)
    rank = jnp.dot(others.astype(jnp.bfloat16), before, preferred_element_type=jnp.float32)
    lane32 = lax.broadcasted_iota(jnp.int32, (32, 128), 1)
    row32 = lax.broadcasted_iota(jnp.int32, (32, 128), 0)
    table = jnp.zeros((32, 128), jnp.float32)
    for r in range(ANC - 1):
        hit = (others > 0.5) & (jnp.abs(rank - float(r)) < 0.5)
        value = jnp.sum(jnp.where(hit, place[0:1, :], 0.0), axis=1, keepdims=True)
        table = jnp.where(lane32 == r, value, table)
    table = jnp.where(lane32 == ANC - 1, jnp.sum(others, axis=1, keepdims=True), table)

    pltpu.make_async_copy(ids_in.at[pl.ds(0, leafs - 1)], ids_in.at[pl.ds(0, leafs - 1)], ids_recv).wait()

    def sources(s, total):
        return total + jnp.where(ids_in[s][0:1, :] == my_start + row32, s.astype(jnp.float32), 0.0)

    source = lax.fori_loop(0, leafs, sources, jnp.zeros((32, 128), jnp.float32))
    table = jnp.where(lane32 == 2 * ANC, source, table)
    mine8 = (lane8 >= my_start) & (owner == me) & (seen8 > 0.5)
    for k in range(EXPORT):
        picked = jnp.sum(
            jnp.where(mine8 & (jnp.abs(rank8 - float(k)) < 0.5), relative, 0.0), axis=1, keepdims=True
        )
        chosen = jnp.sum(
            jnp.where(row32.astype(jnp.float32) == picked[0:1, :], source, 0.0), axis=0, keepdims=True
        )
        table = jnp.where(lane32 == 2 * ANC + 1 + k, chosen, table)
    table_vm[...] = table.astype(jnp.int32)
    to_scalars = pltpu.make_async_copy(table_vm, table_sm, table_sem)
    to_scalars.start()
    to_scalars.wait()

    def find_places(r, carry):
        place_sm[r * ANC] = jnp.clip(table_sm[r, 2 * ANC], 0, leafs - 1)
        for p in range(ANC - 1):
            v = table_sm[r, p]
            near = table_sm[jnp.clip(v, 0, leafs - 1), 2 * ANC]
            place_sm[r * ANC + p + 1] = jnp.clip(jnp.where(v < leafs, near, v), 0, leafs + leafs * EXPORT - 1)
        return carry

    lax.fori_loop(0, SLOTS, find_places, 0)
    my_count = part_ref[me]

    for load in loads:
        load.wait()
    def accumulate(src, c, first):
        wide = pieces[src, c].reshape(rows, feat).astype(jnp.float32)
        gain = gain_vm[src]
        scaled[...] = (wide * gain).astype(jnp.bfloat16)
        part = jnp.sum(wide * wide, axis=1, keepdims=True)
        if first:
            squares[...] = jnp.broadcast_to(part, (rows, 128))
        else:
            squares[...] += jnp.broadcast_to(part, (rows, 128))
        product = jnp.dot(scaled[...], weights[src], preferred_element_type=jnp.float32)
        if first:
            acc[...] = product
        else:
            acc[...] += product

    def slot_copy(o, c):
        peer = lax.rem(me + o, leafs)
        return pltpu.make_async_remote_copy(
            src_ref=send.at[c, peer],
            dst_ref=recv.at[c, me],
            send_sem=slot_send.at[c],
            recv_sem=slot_recv.at[c],
            device_id=(peer, z),
            device_id_type=MESH,
        )

    def slots_arrived(c):
        part = recv.at[c, pl.ds(0, leafs - 1)]
        pltpu.make_async_copy(part, part, slot_recv.at[c]).wait()

    block = core * chips * EXPORT + chip * EXPORT

    def chip_copy(o, c):
        part = far.at[c, pl.ds(block, EXPORT)]
        return pltpu.make_async_remote_copy(
            src_ref=part, dst_ref=part, send_sem=chip_send.at[c], recv_sem=chip_recv.at[c],
            device_id=(lax.rem(chip + o, chips) * 2 + core, z), device_id_type=MESH,
        )

    def chips_arrived(c):
        part = far.at[c, pl.ds(0, (chips - 1) * EXPORT)]
        pltpu.make_async_copy(part, part, chip_recv.at[c]).wait()

    def core_copy(c):
        part = far.at[c, pl.ds(core * chips * EXPORT, chips * EXPORT)]
        return pltpu.make_async_remote_copy(
            src_ref=part, dst_ref=part, send_sem=core_send.at[c], recv_sem=core_recv.at[c],
            device_id=(chip * 2 + 1 - core, z), device_id_type=MESH,
        )

    def core_arrival(c):
        part = far.at[c, pl.ds((1 - core) * chips * EXPORT, chips * EXPORT)]
        return pltpu.make_async_remote_copy(
            src_ref=part, dst_ref=part, send_sem=core_send.at[c], recv_sem=core_recv.at[c],
            device_id=(chip * 2 + 1 - core, z), device_id_type=MESH,
        )

    kv_cols = 2 * k_cols

    def export_start(c):
        slots_arrived(c)

        def keep(s, carry):
            query[c, s] = recv[c, s, :, pl.ds(0, q_cols)]
            pool[c, s] = recv[c, s, :, pl.ds(q_cols, kv_cols)]
            return carry

        lax.fori_loop(0, leafs, keep, 0)
        for k in range(EXPORT):
            far[c, block + k] = pool[c, jnp.clip(table_sm[0, 2 * ANC + 1 + k], 0, leafs - 1)]
        lax.fori_loop(1, chips, lambda o, carry: (chip_copy(o, c).start(), carry)[1], 0)

    def export_core(c):
        chips_arrived(c)
        core_copy(c).start()

    def export_end(c):
        core_arrival(c).wait_recv()

        def keep(s, carry):
            pool[c, leafs + s] = far[c, s]
            return carry

        lax.fori_loop(0, leafs * EXPORT, keep, 0)

    heads = k_cols // HD
    groups = q_cols // k_cols
    q_rows = groups * TOK
    lane = lax.broadcasted_iota(jnp.int32, (1, ANC * TOK), 1)

    tri = lax.broadcasted_iota(jnp.int32, (q_rows, ANC * TOK), 1) <= lax.rem(
        lax.broadcasted_iota(jnp.int32, (q_rows, ANC * TOK), 0), TOK
    )
    tri = tri | (lax.broadcasted_iota(jnp.int32, (q_rows, ANC * TOK), 1) >= TOK)

    def load_queries(own, h, first, last):
        return jnp.concatenate(
            [
                query[c, own, :, pl.ds((h * groups + g) * HD, HD)]
                for c in range(first, last)
                for g in range(groups)
            ],
            axis=0,
        )

    def load_pool(places, column, first, last):
        return jnp.concatenate(
            [pool[c, p, :, pl.ds(column, HD)] for c in range(first, last) for p in places], axis=0
        )

    def attend(q0, q1, k0, k1, final):
        at = pl.ds(q0 * q_rows, (q1 - q0) * q_rows)

        def batch(slots):
            chains = [(n, h) for n in range(len(slots)) for h in range(heads)]
            places = [[place_sm[r * ANC + p] for p in range(ANC)] for r in slots]
            limit = [lane < (table_sm[r, ANC - 1] + 1) * TOK for r in slots]
            past = [x & (lane >= TOK) for x in limit]
            scores = {
                (n, h): lax.dot_general(
                    load_queries(places[n][0], h, q0, q1),
                    load_pool(places[n], h * HD, k0, k1),
                    (((1,), (1,)), ((), ())),
                    preferred_element_type=jnp.float32,
                )
                for n, h in chains
            }
            probs, sums = {}, {}
            for n, h in chains:
                capped = jnp.tanh(scores[n, h] * (query_scale / soft_cap))
                raised = jnp.exp2(capped * (soft_cap * math.log2(math.e)))
                lines, adds = [], []
                for q in range(q0, q1):
                    tiles = []
                    for k in range(k0, k1):
                        tile = raised[
                            (q - q0) * q_rows : (q - q0 + 1) * q_rows,
                            (k - k0) * ANC * TOK : (k - k0 + 1) * ANC * TOK,
                        ]
                        keep = limit[n] if k < q else past[n] if k > q else limit[n] & tri
                        tiles.append(jnp.where(keep, tile, 0.0))
                    lines.append(jnp.concatenate(tiles, axis=1))
                    adds.append(functools.reduce(lambda x, y: x + y, tiles))
                probs[n, h] = jnp.concatenate(lines, axis=0).astype(jnp.bfloat16)
                sums[n, h] = jnp.concatenate(adds, axis=0)
            parts = {
                (n, h): jnp.dot(
                    probs[n, h],
                    load_pool(places[n], k_cols + h * HD, k0, k1),
                    preferred_element_type=jnp.float32,
                )
                for n, h in chains
            }
            if not final:
                for n, h in chains:
                    numer[slots[n], h, at, :] = parts[n, h]
                    total[slots[n], h, at, :] = sums[n, h]
                return
            results = {}
            for n, h in chains:
                whole = jnp.sum(total[slots[n], h] + sums[n, h], axis=1, keepdims=True)
                result = (numer[slots[n], h] + parts[n, h]) * (1.0 / whole)
                results[n, h] = jnp.where(slots[n] < my_count, result, 0.0).astype(jnp.bfloat16)
            for n, h in chains:
                for q in range(CHUNKS):
                    for g in range(groups):
                        start = (q * groups + g) * TOK
                        out_ref[slots[n], pl.ds(q * TOK, TOK), pl.ds((h * groups + g) * HD, HD)] = results[n, h][
                            start : start + TOK
                        ]

        def step(i, carry):
            batch([i * BATCH + n for n in range(BATCH)])
            return carry

        lax.fori_loop(0, SLOTS // BATCH, step, 0)
        if SLOTS % BATCH:
            batch(list(range(SLOTS // BATCH * BATCH, SLOTS)))

    def one_chunk(c, carry):
        accumulate(z, c, True)
        accumulate(left, c, False)
        accumulate(right, c, False)

        for k in range(CHUNKS - 2):

            @pl.when(c == k + 2)
            def _(k=k):
                export_core(k)
                export_end(k)

        @pl.when(c >= 1)
        def _():
            export_start(c - 1)

        forward_arrival(0, c).wait_recv()
        forward_arrival(1, c).wait_recv()
        accumulate(opposite, c, False)

        scale = lax.rsqrt(squares[...] / width + norm_epsilon)
        cosine = angle_cos[c]
        sine = angle_sin[c]
        for head in range(cols // HD):
            at = pl.ds(head * HD, HD)
            value = acc[:, at] * scale
            if head * HD < q_cols + k_cols:
                value = value * cosine + pltpu.roll(value, HD // 2, 1) * sine
            made[:, :, at] = value.astype(jnp.bfloat16).reshape(nodes, TOK, HD)

        def fill(d, carry2):
            send[c, d] = made[index_sm[d]]
            return carry2

        lax.fori_loop(0, leafs, fill, 0)
        lax.fori_loop(1, leafs, lambda o, carry2: (slot_copy(o, c).start(), carry2)[1], 0)
        recv[c, me] = send[c, me]

        @pl.when(c + 1 < CHUNKS)
        def _():
            pass_on(c + 1)


        return carry

    lax.fori_loop(0, CHUNKS, one_chunk, 0)

    last = CHUNKS - 1
    export_core(last - 1)
    export_end(last - 1)
    attend(0, last, 0, last, False)
    export_start(last)
    attend(last, CHUNKS, 0, last, False)
    export_core(last)
    export_end(last)
    attend(0, CHUNKS, last, CHUNKS, True)

    def settle(c, carry):
        for side in (0, 1):
            full(side, 0, c).wait_send()
            full(side, 1, c).wait_send()
            forward(side, c).wait_send()
        sent = send.at[c, pl.ds(0, leafs - 1)]
        pltpu.make_async_copy(sent, sent, slot_send.at[c]).wait()
        exported = far.at[c, pl.ds(0, (chips - 1) * EXPORT)]
        pltpu.make_async_copy(exported, exported, chip_send.at[c]).wait()
        core_copy(c).wait_send()
        return carry

    lax.fori_loop(0, CHUNKS, settle, 0)
    pltpu.make_async_copy(ids_out.at[pl.ds(0, leafs - 1)], ids_out.at[pl.ds(0, leafs - 1)], ids_send).wait()


def on_device(tokens, norm_gain, w_query, w_key, w_value, gen_node, partition, parent, block_mask):
    leafs = lax.axis_size("leaf")
    nodes = gen_node.shape[0]
    feat = tokens.shape[1]
    width = norm_gain.shape[0]
    q_cols = w_query.shape[1]
    k_cols = w_key.shape[1]
    cols = q_cols + 2 * k_cols
    heads = k_cols // HD
    rows = nodes * TOK
    head_rows = q_cols // k_cols * NODE_TOK
    node_total = parent.shape[0]
    half_dim = HD // 2
    inverse_freq = np.exp(
        np.arange(half_dim, dtype=np.float32) * np.float32(-2.0 * math.log(rope_base) / HD)
    ).astype(np.float32)
    freq = jnp.asarray(np.concatenate([inverse_freq, inverse_freq])[None, :])
    bf16, f32, i32 = jnp.bfloat16, jnp.float32, jnp.int32
    dma = pltpu.SemaphoreType.DMA
    smem = pl.BlockSpec(memory_space=pltpu.SMEM)
    vmem = pl.BlockSpec(memory_space=pltpu.VMEM)
    hbm = pl.BlockSpec(memory_space=pl.ANY)
    out = pl.pallas_call(
        functools.partial(fused_kernel, leafs, nodes, width, q_cols, k_cols),
        out_shape=jax.ShapeDtypeStruct((SLOTS, NODE_TOK, q_cols), bf16),
        in_specs=[smem, smem, smem, vmem, vmem, vmem, hbm, hbm, hbm, hbm],
        out_specs=vmem,
        scratch_shapes=[
            pltpu.VMEM((4, CHUNKS, nodes, TOK, feat), bf16),
            pltpu.VMEM((4, feat, cols), bf16),
            pltpu.VMEM((rows, feat), bf16),
            pltpu.VMEM((rows, cols), f32),
            pltpu.VMEM((rows, 128), f32),
            pltpu.VMEM((CHUNKS, rows, HD), f32),
            pltpu.VMEM((CHUNKS, rows, HD), f32),
            pltpu.VMEM((nodes, TOK, cols), bf16),
            pltpu.VMEM((CHUNKS, leafs, TOK, cols), bf16),
            pltpu.VMEM((CHUNKS, leafs, TOK, cols), bf16),
            pltpu.VMEM((CHUNKS, leafs * EXPORT, TOK, 2 * k_cols), bf16),
            pltpu.VMEM((CHUNKS, leafs, TOK, q_cols), bf16),
            pltpu.VMEM((CHUNKS, leafs + leafs * EXPORT, TOK, 2 * k_cols), bf16),
            pltpu.VMEM((SLOTS, heads, head_rows, HD), f32),
            pltpu.VMEM((SLOTS, heads, head_rows, HD), f32),
            pltpu.VMEM((leafs, 8, 128), i32),
            pltpu.VMEM((leafs, 8, 128), i32),
            pltpu.VMEM((32, 128), i32),
            pltpu.VMEM((4, 1, feat), f32),
            pltpu.SMEM((node_total,), i32),
            pltpu.SMEM((leafs,), i32),
            pltpu.SMEM((leafs,), i32),
            pltpu.SMEM((leafs,), i32),
            pltpu.SMEM((32, 128), i32),
            pltpu.SMEM((SLOTS * ANC,), i32),
            dma((3,)),
            dma((CHUNKS,)),
            dma((2, 2, CHUNKS)),
            dma((2, 2, CHUNKS)),
            dma((2, CHUNKS)),
            dma((2, CHUNKS)),
            dma,
            dma,
            dma,
            dma((CHUNKS,)),
            dma((CHUNKS,)),
            dma((CHUNKS,)),
            dma((CHUNKS,)),
            dma((CHUNKS,)),
            dma((CHUNKS,)),
        ],
        compiler_params=pltpu.CompilerParams(
            collective_id=0, has_side_effects=True, vmem_limit_bytes=62 * 1024 * 1024
        ),
        cost_estimate=pl.CostEstimate(
            flops=2 * nodes * NODE_TOK * width * cols, bytes_accessed=30_000_000, transcendentals=0
        ),
        name="tree_attention",
    )(
        gen_node, partition, parent, block_mask, norm_gain, freq,
        tokens.reshape(nodes, NODE_TOK, feat),
        w_query.reshape(4, feat, q_cols), w_key.reshape(4, feat, k_cols), w_value.reshape(4, feat, k_cols),
    )
    return out.reshape(CAP * NODE_TOK, q_cols)


def solution(mesh):
    in_specs = (
        P("leaf", "mp"),
        P(),
        P(None, "mp"),
        P(None, "mp"),
        P(None, "mp"),
        P("leaf"),
        P(),
        P(),
        P(),
    )
    out_specs = P("leaf", "mp")
    return jax.shard_map(
        on_device, mesh=mesh, in_specs=in_specs, out_specs=out_specs, check_vma=False
    )
```

time: 168 us -> 134 us (0.80)
  the two profiles are of different devices: /device:TPU:6 before, /device:TPU:1 now
where the time goes in v2:
time: 134 us
  Pallas kernels  131 us (98%)
  local copies, waits for them, and re-layouts  2.99 us (2%)
    pallas_call x1, Pallas kernels, on_device(): pl.pallas_call(functools.partial(fused_kernel, leafs, nodes, width, q_col...  131 us
    unnamed x1, local copies, waits for them, and re-layouts  2.99 us

profile of v2, /device:TPU:1, one launch (start us, length us, event | category | flops | bytes accessed | tf_op | source)
XLA Modules:
  0.0 133.8 jit_solution(6990280879074374582)
XLA Ops:
  0.0 130.7 %tree_attention.1 = bf16[31,64,512]{2,1,0:T(8,128)(2,1)} custom-call(s32[16]{0:T(128)} %gen_ref.1, s32[32]{0:T(128)} %part_ref.1, s32[512]{0:T(512)} %parent_ref.1, s32[512,512]{1,0:T(8,128)} %mask_ref.1, bf16[4608]{0:T(1024)(128)(2,1)} %gain_ref.1, f32[1,128]{1,0:T(1,128)} %constant.2.clone.freq_ref, bf16[16,64,1152]{2,1,0:T(8,128)(2,1)} %bitcast.7, ...), custom_call_target="tpu_custom_call" | custom-call | flops 9663676416 | bytes 30000000 | tf_op jit(solution)/shard_map/tree_attention/pallas_call | solution.py:569
  130.8 3.0 %copy.12 = bf16[1984,512]{1,0:T(8,128)(2,1)} copy(bf16[1984,512]{1,0:T(8,128)(2,1)} %bitcast.5) | data formatting | bytes 4063232

commit v3 on v2

--- a/solution.py
+++ b/solution.py
@@ -17,7 +17,9 @@
 NODE_TOK = 64
 TOK = NODE_TOK // CHUNKS
 SLOTS = CAP
-BATCH = 4
+BATCH = 8
+CHIP_STEPS = [(2, 2), (0, 1), (1, 0), (0, 3), (3, 0), (2, 1), (1, 2), (2, 3), (3, 2), (0, 2), (2, 0), (1, 1), (3, 3), (1, 3), (3, 1)]
+SLOT_STEPS = [(2, 2, 0), (0, 1, 0), (1, 0, 0), (0, 3, 0), (3, 0, 0), (2, 1, 0), (1, 2, 0), (2, 3, 0), (3, 2, 0), (0, 2, 0), (2, 0, 0), (1, 1, 0), (3, 3, 0), (1, 3, 0), (3, 1, 0), (2, 2, 1), (0, 1, 1), (1, 0, 1), (0, 3, 1), (3, 0, 1), (2, 1, 1), (1, 2, 1), (2, 3, 1), (3, 2, 1), (0, 2, 1), (2, 0, 1), (1, 1, 1), (3, 3, 1), (1, 3, 1), (3, 1, 1), (0, 0, 1)]
 
 norm_epsilon = 1e-06
 soft_cap = 50.0
@@ -31,11 +33,11 @@
     leafs, nodes, width, q_cols, k_cols,
     gen_ref, part_ref, parent_ref, mask_ref, gain_ref, freq_ref, tok_ref, wq_ref, wk_ref, wv_ref,
     out_ref,
-    pieces, weights, scaled, acc, squares, angle_cos, angle_sin, made, send, recv, far,
+    pieces, weights, scaled, acc, squares, angle_cos, angle_sin, made, send_kv, send_q, recv_kv, recv_q, far,
     query, pool, numer, total, ids_out, ids_in, table_vm, gain_vm,
     depth_sm, index_sm, start_sm, end_sm, table_sm, place_sm,
     load_sem, own_sem, full_send, full_recv, half_send, half_recv, ids_send, ids_recv, table_sem,
-    slot_send, slot_recv, chip_send, chip_recv, core_send, core_recv,
+    kv_send, kv_recv, q_send, q_recv, chip_send, chip_recv, core_send, core_recv,
 ):
     me = lax.axis_index("leaf")
     z = lax.axis_index("mp")
@@ -51,6 +53,10 @@
     chip = lax.div(me, 2)
     chips = leafs // 2
 
+    def chip_at(dy, dx):
+        return lax.rem(lax.div(chip, 4) + dy, chips // 4) * 4 + lax.rem(lax.rem(chip, 4) + dx, 4)
+
+
     loads = [
         pltpu.make_async_copy(wq_ref, weights.at[:, :, pl.ds(0, q_cols)], load_sem.at[0]),
         pltpu.make_async_copy(wk_ref, weights.at[:, :, pl.ds(q_cols, k_cols)], load_sem.at[1]),
@@ -130,7 +136,7 @@
                 for side in (0, 1):
                     full(side, side ^ step, 0).start()
 
-    def pass_on(c):
+    def pass_on(c, between=None):
         for side in (0, 1):
             full_arrival(side, side, c).wait_recv()
             forward(side, c).start()
@@ -140,6 +146,8 @@
             for side in (0, 1):
                 full(side, side, c + 1).start()
 
+        if between is not None:
+            between()
         for side in (0, 1):
             full_arrival(side, 1 - side, c).wait_recv()
 
@@ -301,34 +309,36 @@
             squares[...] = jnp.broadcast_to(part, (rows, 128))
         else:
             squares[...] += jnp.broadcast_to(part, (rows, 128))
+        if src is opposite:
+            return
         product = jnp.dot(scaled[...], weights[src], preferred_element_type=jnp.float32)
         if first:
             acc[...] = product
         else:
             acc[...] += product
 
-    def slot_copy(o, c):
-        peer = lax.rem(me + o, leafs)
-        return pltpu.make_async_remote_copy(
-            src_ref=send.at[c, peer],
-            dst_ref=recv.at[c, me],
-            send_sem=slot_send.at[c],
-            recv_sem=slot_recv.at[c],
+    def slot_copy(step, c, source, target, sent, arrived):
+        peer = chip_at(step[0], step[1]) * 2 + lax.rem(core + step[2], 2)
+        return pltpu.make_async_remote_copy(
+            src_ref=source.at[c, peer],
+            dst_ref=target.at[c, me],
+            send_sem=sent.at[c],
+            recv_sem=arrived.at[c],
             device_id=(peer, z),
             device_id_type=MESH,
         )
 
-    def slots_arrived(c):
-        part = recv.at[c, pl.ds(0, leafs - 1)]
-        pltpu.make_async_copy(part, part, slot_recv.at[c]).wait()
+    def all_slots(buffer, c, sem):
+        part = buffer.at[c, pl.ds(0, leafs - 1)]
+        pltpu.make_async_copy(part, part, sem.at[c]).wait()
 
     block = core * chips * EXPORT + chip * EXPORT
 
-    def chip_copy(o, c):
+    def chip_copy(step, c):
         part = far.at[c, pl.ds(block, EXPORT)]
         return pltpu.make_async_remote_copy(
             src_ref=part, dst_ref=part, send_sem=chip_send.at[c], recv_sem=chip_recv.at[c],
-            device_id=(lax.rem(chip + o, chips) * 2 + core, z), device_id_type=MESH,
+            device_id=(chip_at(step[0], step[1]) * 2 + core, z), device_id_type=MESH,
         )
 
     def chips_arrived(c):
@@ -352,17 +362,28 @@
     kv_cols = 2 * k_cols
 
     def export_start(c):
-        slots_arrived(c)
-
-        def keep(s, carry):
-            query[c, s] = recv[c, s, :, pl.ds(0, q_cols)]
-            pool[c, s] = recv[c, s, :, pl.ds(q_cols, kv_cols)]
+        all_slots(recv_kv, c, kv_recv)
+
+        def keep(i, carry):
+            for n in range(4):
+                pool[c, i * 4 + n] = recv_kv[c, i * 4 + n]
             return carry
 
-        lax.fori_loop(0, leafs, keep, 0)
+        lax.fori_loop(0, leafs // 4, keep, 0)
         for k in range(EXPORT):
             far[c, block + k] = pool[c, jnp.clip(table_sm[0, 2 * ANC + 1 + k], 0, leafs - 1)]
-        lax.fori_loop(1, chips, lambda o, carry: (chip_copy(o, c).start(), carry)[1], 0)
+        for step in CHIP_STEPS:
+            chip_copy(step, c).start()
+
+    def keep_queries(c):
+        all_slots(recv_q, c, q_recv)
+
+        def keep(i, carry):
+            for n in range(4):
+                query[c, i * 4 + n] = recv_q[c, i * 4 + n]
+            return carry
+
+        lax.fori_loop(0, leafs // 4, keep, 0)
 
     def export_core(c):
         chips_arrived(c)
@@ -371,11 +392,12 @@
     def export_end(c):
         core_arrival(c).wait_recv()
 
-        def keep(s, carry):
-            pool[c, leafs + s] = far[c, s]
+        def keep(i, carry):
+            for n in range(4):
+                pool[c, leafs + i * 4 + n] = far[c, i * 4 + n]
             return carry
 
-        lax.fori_loop(0, leafs * EXPORT, keep, 0)
+        lax.fori_loop(0, leafs * EXPORT // 4, keep, 0)
 
     heads = k_cols // HD
     groups = q_cols // k_cols
@@ -485,7 +507,7 @@
 
         @pl.when(c >= 1)
         def _():
-            export_start(c - 1)
+            keep_queries(c - 1)
 
         forward_arrival(0, c).wait_recv()
         forward_arrival(1, c).wait_recv()
@@ -494,25 +516,33 @@
         scale = lax.rsqrt(squares[...] / width + norm_epsilon)
         cosine = angle_cos[c]
         sine = angle_sin[c]
-        for head in range(cols // HD):
-            at = pl.ds(head * HD, HD)
-            value = acc[:, at] * scale
-            if head * HD < q_cols + k_cols:
-                value = value * cosine + pltpu.roll(value, HD // 2, 1) * sine
-            made[:, :, at] = value.astype(jnp.bfloat16).reshape(nodes, TOK, HD)
-
-        def fill(d, carry2):
-            send[c, d] = made[index_sm[d]]
-            return carry2
-
-        lax.fori_loop(0, leafs, fill, 0)
-        lax.fori_loop(1, leafs, lambda o, carry2: (slot_copy(o, c).start(), carry2)[1], 0)
-        recv[c, me] = send[c, me]
+
+        def finish(first, count, target, buffer, sent, arrived):
+            at = pl.ds(first, count)
+            acc[:, at] += jnp.dot(scaled[...], weights[opposite, :, at], preferred_element_type=jnp.float32)
+            for column in range(first, first + count, HD):
+                value = acc[:, pl.ds(column, HD)] * scale
+                if column < q_cols + k_cols:
+                    value = value * cosine + pltpu.roll(value, HD // 2, 1) * sine
+                made[:, :, pl.ds(column, HD)] = value.astype(jnp.bfloat16).reshape(nodes, TOK, HD)
+
+            def fill(i, carry2):
+                for n in range(4):
+                    d = i * 4 + n
+                    target[c, d] = made[index_sm[d], :, at]
+                return carry2
+
+            lax.fori_loop(0, leafs // 4, fill, 0)
+            for step in SLOT_STEPS:
+                slot_copy(step, c, target, buffer, sent, arrived).start()
+            buffer[c, me] = target[c, me]
+
+        finish(q_cols, 2 * k_cols, send_kv, recv_kv, kv_send, kv_recv)
+        finish(0, q_cols, send_q, recv_q, q_send, q_recv)
 
         @pl.when(c + 1 < CHUNKS)
         def _():
-            pass_on(c + 1)
-
+            pass_on(c + 1, lambda: export_start(c))
 
         return carry
 
@@ -523,6 +553,7 @@
     export_end(last - 1)
     attend(0, last, 0, last, False)
     export_start(last)
+    keep_queries(last)
     attend(last, CHUNKS, 0, last, False)
     export_core(last)
     export_end(last)
@@ -533,8 +564,8 @@
             full(side, 0, c).wait_send()
             full(side, 1, c).wait_send()
             forward(side, c).wait_send()
-        sent = send.at[c, pl.ds(0, leafs - 1)]
-        pltpu.make_async_copy(sent, sent, slot_send.at[c]).wait()
+        all_slots(send_kv, c, kv_send)
+        all_slots(send_q, c, q_send)
         exported = far.at[c, pl.ds(0, (chips - 1) * EXPORT)]
         pltpu.make_async_copy(exported, exported, chip_send.at[c]).wait()
         core_copy(c).wait_send()
@@ -580,8 +611,10 @@
             pltpu.VMEM((CHUNKS, rows, HD), f32),
             pltpu.VMEM((CHUNKS, rows, HD), f32),
             pltpu.VMEM((nodes, TOK, cols), bf16),
-            pltpu.VMEM((CHUNKS, leafs, TOK, cols), bf16),
-            pltpu.VMEM((CHUNKS, leafs, TOK, cols), bf16),
+            pltpu.VMEM((CHUNKS, leafs, TOK, 2 * k_cols), bf16),
+            pltpu.VMEM((CHUNKS, leafs, TOK, q_cols), bf16),
+            pltpu.VMEM((CHUNKS, leafs, TOK, 2 * k_cols), bf16),
+            pltpu.VMEM((CHUNKS, leafs, TOK, q_cols), bf16),
             pltpu.VMEM((CHUNKS, leafs * EXPORT, TOK, 2 * k_cols), bf16),
             pltpu.VMEM((CHUNKS, leafs, TOK, q_cols), bf16),
             pltpu.VMEM((CHUNKS, leafs + leafs * EXPORT, TOK, 2 * k_cols), bf16),
@@ -612,6 +645,8 @@
             dma((CHUNKS,)),
             dma((CHUNKS,)),
             dma((CHUNKS,)),
+            dma((CHUNKS,)),
+            dma((CHUNKS,)),
         ],
         compiler_params=pltpu.CompilerParams(
             collective_id=0, has_side_effects=True, vmem_limit_bytes=62 * 1024 * 1024

time: 134 us -> 119 us (0.89)
  Pallas kernels: 131 us -> 116 us
    pallas_call x1, Pallas kernels: 131 us -> 116 us  [on_device(): pl.pallas_call(functools.partial(fused_kernel, leafs, nodes, width, q_col...]
where the time goes in v3:
time: 119 us
  Pallas kernels  116 us (97%)
  local copies, waits for them, and re-layouts  2.99 us (3%)
    pallas_call x1, Pallas kernels, on_device(): pl.pallas_call(functools.partial(fused_kernel, leafs, nodes, width, q_col...  116 us
    unnamed x1, local copies, waits for them, and re-layouts  2.99 us

profile of v3, /device:TPU:1, one launch (start us, length us, event | category | flops | bytes accessed | tf_op | source)
XLA Modules:
  0.0 118.8 jit_solution(3265326374527530250)
XLA Ops:
  0.0 115.8 %tree_attention.1 = bf16[31,64,512]{2,1,0:T(8,128)(2,1)} custom-call(s32[16]{0:T(128)} %gen_ref.1, s32[32]{0:T(128)} %part_ref.1, s32[512]{0:T(512)} %parent_ref.1, s32[512,512]{1,0:T(8,128)} %mask_ref.1, bf16[4608]{0:T(1024)(128)(2,1)} %gain_ref.1, f32[1,128]{1,0:T(1,128)} %constant.2.clone.freq_ref, bf16[16,64,1152]{2,1,0:T(8,128)(2,1)} %bitcast.7, ...), custom_call_target="tpu_custom_call" | custom-call | flops 9663676416 | bytes 30000000 | tf_op jit(solution)/shard_map/tree_attention/pallas_call | solution.py:600
  115.8 3.0 %copy.12 = bf16[1984,512]{1,0:T(8,128)(2,1)} copy(bf16[1984,512]{1,0:T(8,128)(2,1)} %bitcast.5) | data formatting | bytes 4063232

commit v4 on v2

--- a/solution.py
+++ b/solution.py
@@ -16,8 +16,13 @@
 CHUNKS = 4
 NODE_TOK = 64
 TOK = NODE_TOK // CHUNKS
+SUBS = 2 * CHUNKS
+SUB = TOK // 2
 SLOTS = CAP
-BATCH = 4
+BATCH = 8
+OUT_PARTS = 8
+CHIP_STEPS = [(2, 2), (0, 1), (1, 0), (0, 3), (3, 0), (2, 1), (1, 2), (2, 3), (3, 2), (0, 2), (2, 0), (1, 1), (3, 3), (1, 3), (3, 1)]
+SLOT_STEPS = [(2, 2, 0), (0, 1, 0), (1, 0, 0), (0, 3, 0), (3, 0, 0), (2, 1, 0), (1, 2, 0), (2, 3, 0), (3, 2, 0), (0, 2, 0), (2, 0, 0), (1, 1, 0), (3, 3, 0), (1, 3, 0), (3, 1, 0), (2, 2, 1), (0, 1, 1), (1, 0, 1), (0, 3, 1), (3, 0, 1), (2, 1, 1), (1, 2, 1), (2, 3, 1), (3, 2, 1), (0, 2, 1), (2, 0, 1), (1, 1, 1), (3, 3, 1), (1, 3, 1), (3, 1, 1), (0, 0, 1)]
 
 norm_epsilon = 1e-06
 soft_cap = 50.0
@@ -31,7 +36,7 @@
     leafs, nodes, width, q_cols, k_cols,
     gen_ref, part_ref, parent_ref, mask_ref, gain_ref, freq_ref, tok_ref, wq_ref, wk_ref, wv_ref,
     out_ref,
-    pieces, weights, scaled, acc, squares, angle_cos, angle_sin, made, send, recv, far,
+    held, pieces, weights, scaled, acc, squares, angle_cos, angle_sin, made, send, recv, near, far,
     query, pool, numer, total, ids_out, ids_in, table_vm, gain_vm,
     depth_sm, index_sm, start_sm, end_sm, table_sm, place_sm,
     load_sem, own_sem, full_send, full_recv, half_send, half_recv, ids_send, ids_recv, table_sem,
@@ -43,13 +48,17 @@
     right, left = lax.rem(z + 1, mp), lax.rem(z + 3, mp)
     opposite = lax.rem(z + 2, mp)
     feat = width // mp
-    rows = nodes * TOK
+    rows = nodes * SUB
     cols = q_cols + 2 * k_cols
-    half = nodes // 2
+    half = nodes // 4
     node_total = parent_ref.shape[0]
     core = lax.rem(me, 2)
     chip = lax.div(me, 2)
     chips = leafs // 2
+
+    def chip_at(dy, dx):
+        return lax.rem(lax.div(chip, 4) + dy, chips // 4) * 4 + lax.rem(lax.rem(chip, 4) + dx, 4)
+
 
     loads = [
         pltpu.make_async_copy(wq_ref, weights.at[:, :, pl.ds(0, q_cols)], load_sem.at[0]),
@@ -58,9 +67,20 @@
     ]
 
     def own_load(c):
-        return pltpu.make_async_copy(
-            tok_ref.at[:, pl.ds(pl.multiple_of(c * TOK, TOK), TOK), :], pieces.at[z, c], own_sem.at[c]
-        )
+        at = pl.ds(pl.multiple_of(c * TOK, TOK), TOK)
+        return pltpu.make_async_copy(tok_ref.at[:, at, :], held.at[:, at, :], own_sem.at[c])
+
+    def deal(c):
+        at = pl.ds(pl.multiple_of(c * TOK, TOK), TOK)
+
+        def pair(j, carry):
+            one = held[2 * j, at, :].astype(jnp.float32)
+            two = held[2 * j + 1, at, :].astype(jnp.float32)
+            pieces[z, 2 * c, j] = jnp.concatenate([one[:SUB], two[:SUB]], axis=0).astype(jnp.bfloat16)
+            pieces[z, 2 * c + 1, j] = jnp.concatenate([one[SUB:], two[SUB:]], axis=0).astype(jnp.bfloat16)
+            return carry
+
+        lax.fori_loop(0, nodes // 2, pair, 0)
 
     barrier = pltpu.get_barrier_semaphore()
 
@@ -125,25 +145,29 @@
 
     for c in range(CHUNKS):
         own_load(c).wait()
+    for c in range(CHUNKS):
+        deal(c)
         if c == 0:
             for step in (0, 1):
                 for side in (0, 1):
                     full(side, side ^ step, 0).start()
 
-    def pass_on(c):
+    def pass_on(c, between=None):
         for side in (0, 1):
             full_arrival(side, side, c).wait_recv()
             forward(side, c).start()
 
-        @pl.when(c + 1 < CHUNKS)
+        @pl.when(c + 1 < SUBS)
         def _():
             for side in (0, 1):
                 full(side, side, c + 1).start()
 
+        if between is not None:
+            between()
         for side in (0, 1):
             full_arrival(side, 1 - side, c).wait_recv()
 
-        @pl.when(c + 1 < CHUNKS)
+        @pl.when(c + 1 < SUBS)
         def _():
             for side in (0, 1):
                 full(side, 1 - side, c + 1).start()
@@ -190,13 +214,13 @@
 
     pass_on(jnp.int32(0))
 
-    token_row = lax.broadcasted_iota(jnp.int32, (TOK, HD), 0)
+    token_row = lax.broadcasted_iota(jnp.int32, (SUB, HD), 0)
     sign = jnp.where(lax.broadcasted_iota(jnp.int32, (rows, HD), 1) < HD // 2, -1.0, 1.0)
 
     def tables(c, carry):
         def one_node(b, carry2):
-            position = depth_sm[gen_ref[b]] * NODE_TOK + c * TOK + token_row
-            at = pl.ds(pl.multiple_of(b * TOK, TOK), TOK)
+            position = depth_sm[gen_ref[b]] * NODE_TOK + c * SUB + token_row
+            at = pl.ds(pl.multiple_of(b * SUB, SUB), SUB)
             angle_cos[c, at, :] = position.astype(jnp.float32) * freq_ref[...]
             return carry2
 
@@ -206,7 +230,7 @@
         angle_cos[c] = jnp.cos(angles)
         return carry
 
-    lax.fori_loop(0, CHUNKS, tables, 0)
+    lax.fori_loop(0, SUBS, tables, 0)
 
     lane8 = lax.broadcasted_iota(jnp.int32, (8, node_total), 1)
 
@@ -301,14 +325,16 @@
             squares[...] = jnp.broadcast_to(part, (rows, 128))
         else:
             squares[...] += jnp.broadcast_to(part, (rows, 128))
+        if src is opposite:
+            return
         product = jnp.dot(scaled[...], weights[src], preferred_element_type=jnp.float32)
         if first:
             acc[...] = product
         else:
             acc[...] += product
 
-    def slot_copy(o, c):
-        peer = lax.rem(me + o, leafs)
+    def slot_copy(step, c):
+        peer = chip_at(step[0], step[1]) * 2 + lax.rem(core + step[2], 2)
         return pltpu.make_async_remote_copy(
             src_ref=send.at[c, peer],
             dst_ref=recv.at[c, me],
@@ -318,32 +344,32 @@
             device_id_type=MESH,
         )
 
-    def slots_arrived(c):
-        part = recv.at[c, pl.ds(0, leafs - 1)]
-        pltpu.make_async_copy(part, part, slot_recv.at[c]).wait()
-
-    block = core * chips * EXPORT + chip * EXPORT
-
-    def chip_copy(o, c):
-        part = far.at[c, pl.ds(block, EXPORT)]
+    def all_slots(buffer, c, sem):
+        part = buffer.at[c, pl.ds(0, leafs - 1)]
+        pltpu.make_async_copy(part, part, sem.at[c]).wait()
+
+    place = core * chips + chip
+
+    def chip_copy(step, c):
+        part = far.at[c, place]
         return pltpu.make_async_remote_copy(
             src_ref=part, dst_ref=part, send_sem=chip_send.at[c], recv_sem=chip_recv.at[c],
-            device_id=(lax.rem(chip + o, chips) * 2 + core, z), device_id_type=MESH,
+            device_id=(chip_at(step[0], step[1]) * 2 + core, z), device_id_type=MESH,
         )
 
     def chips_arrived(c):
-        part = far.at[c, pl.ds(0, (chips - 1) * EXPORT)]
+        part = far.at[c, pl.ds(0, chips - 1)]
         pltpu.make_async_copy(part, part, chip_recv.at[c]).wait()
 
     def core_copy(c):
-        part = far.at[c, pl.ds(core * chips * EXPORT, chips * EXPORT)]
+        part = far.at[c, pl.ds(core * chips, chips)]
         return pltpu.make_async_remote_copy(
             src_ref=part, dst_ref=part, send_sem=core_send.at[c], recv_sem=core_recv.at[c],
             device_id=(chip * 2 + 1 - core, z), device_id_type=MESH,
         )
 
     def core_arrival(c):
-        part = far.at[c, pl.ds((1 - core) * chips * EXPORT, chips * EXPORT)]
+        part = far.at[c, pl.ds((1 - core) * chips, chips)]
         return pltpu.make_async_remote_copy(
             src_ref=part, dst_ref=part, send_sem=core_send.at[c], recv_sem=core_recv.at[c],
             device_id=(chip * 2 + 1 - core, z), device_id_type=MESH,
@@ -352,30 +378,56 @@
     kv_cols = 2 * k_cols
 
     def export_start(c):
-        slots_arrived(c)
-
-        def keep(s, carry):
-            query[c, s] = recv[c, s, :, pl.ds(0, q_cols)]
-            pool[c, s] = recv[c, s, :, pl.ds(q_cols, kv_cols)]
+        all_slots(recv, c, slot_recv)
+
+        def keep(i, carry):
+            for n in range(4):
+                near[i * 4 + n] = recv[c, i * 4 + n]
             return carry
 
-        lax.fori_loop(0, leafs, keep, 0)
-        for k in range(EXPORT):
-            far[c, block + k] = pool[c, jnp.clip(table_sm[0, 2 * ANC + 1 + k], 0, leafs - 1)]
-        lax.fori_loop(1, chips, lambda o, carry: (chip_copy(o, c).start(), carry)[1], 0)
+        lax.fori_loop(0, leafs // 4, keep, 0)
+        exported = [
+            near[jnp.clip(table_sm[0, 2 * ANC + 1 + k], 0, leafs - 1)].astype(jnp.float32)[:SUB]
+            for k in range(EXPORT)
+        ]
+        far[c, place] = jnp.concatenate(exported, axis=0).astype(jnp.bfloat16)
+        for step in CHIP_STEPS:
+            chip_copy(step, c).start()
+
+    def join(even, odd, k):
+        at = slice(k * SUB, (k + 1) * SUB)
+        return jnp.concatenate([even[at], odd[at]], axis=0).astype(jnp.bfloat16)
+
+    def gather_near(c):
+        def keep(i, carry):
+            for n in range(2):
+                s = i * 2 + n
+                even, odd = recv[2 * c, s].astype(jnp.float32), recv[2 * c + 1, s].astype(jnp.float32)
+                pool[c, s] = join(even, odd, 0)
+                query[c, s] = join(even, odd, 1)
+            return carry
+
+        lax.fori_loop(0, leafs // 2, keep, 0)
+
+    def gather_far(c):
+        def keep(i, carry):
+            for n in range(2):
+                s = i * 2 + n
+                even, odd = far[2 * c, s].astype(jnp.float32), far[2 * c + 1, s].astype(jnp.float32)
+                for k in range(EXPORT):
+                    pool[c, leafs + s * EXPORT + k] = join(even, odd, k)
+            return carry
+
+        lax.fori_loop(0, leafs // 2, keep, 0)
 
     def export_core(c):
         chips_arrived(c)
         core_copy(c).start()
 
     def export_end(c):
-        core_arrival(c).wait_recv()
-
-        def keep(s, carry):
-            pool[c, leafs + s] = far[c, s]
-            return carry
-
-        lax.fori_loop(0, leafs * EXPORT, keep, 0)
+        core_arrival(2 * c).wait_recv()
+        core_arrival(2 * c + 1).wait_recv()
+        gather_far(c)
 
     heads = k_cols // HD
     groups = q_cols // k_cols
@@ -463,13 +515,15 @@
                             start : start + TOK
                         ]
 
+        whole, rest = SLOTS // BATCH, SLOTS % BATCH
+
         def step(i, carry):
             batch([i * BATCH + n for n in range(BATCH)])
             return carry
 
-        lax.fori_loop(0, SLOTS // BATCH, step, 0)
-        if SLOTS % BATCH:
-            batch(list(range(SLOTS // BATCH * BATCH, SLOTS)))
+        lax.fori_loop(0, whole, step, 0)
+        if rest:
+            batch(list(range(whole * BATCH, SLOTS)))
 
     def one_chunk(c, carry):
         accumulate(z, c, True)
@@ -478,53 +532,67 @@
 
         for k in range(CHUNKS - 2):
 
-            @pl.when(c == k + 2)
+            @pl.when(c == 2 * k + 4)
             def _(k=k):
-                export_core(k)
+                gather_near(k)
                 export_end(k)
+
+        forward_arrival(0, c).wait_recv()
+        forward_arrival(1, c).wait_recv()
+        accumulate(opposite, c, False)
+
+        scale = lax.rsqrt(squares[...] / width + norm_epsilon)
+        cosine = angle_cos[c]
+        sine = angle_sin[c]
+
+        acc[...] += jnp.dot(scaled[...], weights[opposite], preferred_element_type=jnp.float32)
+
+        def head(column):
+            value = acc[:, pl.ds(column, HD)] * scale
+            if column < q_cols + k_cols:
+                value = value * cosine + pltpu.roll(value, HD // 2, 1) * sine
+            return value.reshape(nodes, SUB, HD)
+
+        for column in range(0, q_cols, HD):
+            both = jnp.concatenate([head(q_cols + column), head(column)], axis=1)
+            made[:, :, pl.ds(column, HD)] = both.astype(jnp.bfloat16)
+
+        def fill(i, carry2):
+            for n in range(4):
+                d = i * 4 + n
+                send[c, d] = made[index_sm[d]]
+            return carry2
+
+        lax.fori_loop(0, leafs // 4, fill, 0)
+        for step in SLOT_STEPS:
+            slot_copy(step, c).start()
+        recv[c, me] = send[c, me]
 
         @pl.when(c >= 1)
         def _():
             export_start(c - 1)
 
-        forward_arrival(0, c).wait_recv()
-        forward_arrival(1, c).wait_recv()
-        accumulate(opposite, c, False)
-
-        scale = lax.rsqrt(squares[...] / width + norm_epsilon)
-        cosine = angle_cos[c]
-        sine = angle_sin[c]
-        for head in range(cols // HD):
-            at = pl.ds(head * HD, HD)
-            value = acc[:, at] * scale
-            if head * HD < q_cols + k_cols:
-                value = value * cosine + pltpu.roll(value, HD // 2, 1) * sine
-            made[:, :, at] = value.astype(jnp.bfloat16).reshape(nodes, TOK, HD)
-
-        def fill(d, carry2):
-            send[c, d] = made[index_sm[d]]
-            return carry2
-
-        lax.fori_loop(0, leafs, fill, 0)
-        lax.fori_loop(1, leafs, lambda o, carry2: (slot_copy(o, c).start(), carry2)[1], 0)
-        recv[c, me] = send[c, me]
-
-        @pl.when(c + 1 < CHUNKS)
+        @pl.when(c >= 2)
+        def _():
+            export_core(c - 2)
+
+        @pl.when(c + 1 < SUBS)
         def _():
             pass_on(c + 1)
 
-
         return carry
 
-    lax.fori_loop(0, CHUNKS, one_chunk, 0)
+    lax.fori_loop(0, SUBS, one_chunk, 0)
 
     last = CHUNKS - 1
-    export_core(last - 1)
+    gather_near(last - 1)
     export_end(last - 1)
     attend(0, last, 0, last, False)
-    export_start(last)
+    export_start(SUBS - 1)
+    export_core(SUBS - 2)
+    gather_near(last)
     attend(last, CHUNKS, 0, last, False)
-    export_core(last)
+    export_core(SUBS - 1)
     export_end(last)
     attend(0, CHUNKS, last, CHUNKS, True)
 
@@ -533,15 +601,28 @@
             full(side, 0, c).wait_send()
             full(side, 1, c).wait_send()
             forward(side, c).wait_send()
-        sent = send.at[c, pl.ds(0, leafs - 1)]
-        pltpu.make_async_copy(sent, sent, slot_send.at[c]).wait()
-        exported = far.at[c, pl.ds(0, (chips - 1) * EXPORT)]
+        all_slots(send, c, slot_send)
+        exported = far.at[c, pl.ds(0, chips - 1)]
         pltpu.make_async_copy(exported, exported, chip_send.at[c]).wait()
         core_copy(c).wait_send()
         return carry
 
-    lax.fori_loop(0, CHUNKS, settle, 0)
+    lax.fori_loop(0, SUBS, settle, 0)
     pltpu.make_async_copy(ids_out.at[pl.ds(0, leafs - 1)], ids_out.at[pl.ds(0, leafs - 1)], ids_send).wait()
+
+
+def hand_over(from_ref, to_ref, held, in_sems, out_sems):
+    size = -(-SLOTS // OUT_PARTS)
+    spans = [pl.ds(i * size, min(size, SLOTS - i * size)) for i in range(OUT_PARTS)]
+    loads = [pltpu.make_async_copy(from_ref.at[at], held.at[at], in_sems.at[i]) for i, at in enumerate(spans)]
+    stores = [pltpu.make_async_copy(held.at[at], to_ref.at[at], out_sems.at[i]) for i, at in enumerate(spans)]
+    for load in loads:
+        load.start()
+    for load, store in zip(loads, stores):
+        load.wait()
+        store.start()
+    for store in stores:
+        store.wait()
 
 
 def on_device(tokens, norm_gain, w_query, w_key, w_value, gen_node, partition, parent, block_mask):
@@ -553,7 +634,7 @@
     k_cols = w_key.shape[1]
     cols = q_cols + 2 * k_cols
     heads = k_cols // HD
-    rows = nodes * TOK
+    rows = nodes * SUB
     head_rows = q_cols // k_cols * NODE_TOK
     node_total = parent.shape[0]
     half_dim = HD // 2
@@ -572,17 +653,19 @@
         in_specs=[smem, smem, smem, vmem, vmem, vmem, hbm, hbm, hbm, hbm],
         out_specs=vmem,
         scratch_shapes=[
-            pltpu.VMEM((4, CHUNKS, nodes, TOK, feat), bf16),
+            pltpu.VMEM((nodes, NODE_TOK, feat), bf16),
+            pltpu.VMEM((4, SUBS, nodes // 2, TOK, feat), bf16),
             pltpu.VMEM((4, feat, cols), bf16),
             pltpu.VMEM((rows, feat), bf16),
             pltpu.VMEM((rows, cols), f32),
             pltpu.VMEM((rows, 128), f32),
-            pltpu.VMEM((CHUNKS, rows, HD), f32),
-            pltpu.VMEM((CHUNKS, rows, HD), f32),
-            pltpu.VMEM((nodes, TOK, cols), bf16),
-            pltpu.VMEM((CHUNKS, leafs, TOK, cols), bf16),
-            pltpu.VMEM((CHUNKS, leafs, TOK, cols), bf16),
-            pltpu.VMEM((CHUNKS, leafs * EXPORT, TOK, 2 * k_cols), bf16),
+            pltpu.VMEM((SUBS, rows, HD), f32),
+            pltpu.VMEM((SUBS, rows, HD), f32),
+            pltpu.VMEM((nodes, TOK, q_cols), bf16),
+            pltpu.VMEM((SUBS, leafs, TOK, q_cols), bf16),
+            pltpu.VMEM((SUBS, leafs, TOK, q_cols), bf16),
+            pltpu.VMEM((leafs, TOK, q_cols), bf16),
+            pltpu.VMEM((SUBS, leafs, TOK, 2 * k_cols), bf16),
             pltpu.VMEM((CHUNKS, leafs, TOK, q_cols), bf16),
             pltpu.VMEM((CHUNKS, leafs + leafs * EXPORT, TOK, 2 * k_cols), bf16),
             pltpu.VMEM((SLOTS, heads, head_rows, HD), f32),
@@ -599,19 +682,19 @@
             pltpu.SMEM((SLOTS * ANC,), i32),
             dma((3,)),
             dma((CHUNKS,)),
-            dma((2, 2, CHUNKS)),
-            dma((2, 2, CHUNKS)),
-            dma((2, CHUNKS)),
-            dma((2, CHUNKS)),
+            dma((2, 2, SUBS)),
+            dma((2, 2, SUBS)),
+            dma((2, SUBS)),
+            dma((2, SUBS)),
             dma,
             dma,
             dma,
-            dma((CHUNKS,)),
-            dma((CHUNKS,)),
-            dma((CHUNKS,)),
-            dma((CHUNKS,)),
-            dma((CHUNKS,)),
-            dma((CHUNKS,)),
+            dma((SUBS,)),
+            dma((SUBS,)),
+            dma((SUBS,)),
+            dma((SUBS,)),
+            dma((SUBS,)),
+            dma((SUBS,)),
         ],
         compiler_params=pltpu.CompilerParams(
             collective_id=0, has_side_effects=True, vmem_limit_bytes=62 * 1024 * 1024
@@ -625,7 +708,14 @@
         tokens.reshape(nodes, NODE_TOK, feat),
         w_query.reshape(4, feat, q_cols), w_key.reshape(4, feat, k_cols), w_value.reshape(4, feat, k_cols),
     )
-    return out.reshape(CAP * NODE_TOK, q_cols)
+    return pl.pallas_call(
+        hand_over,
+        out_shape=jax.ShapeDtypeStruct((SLOTS, NODE_TOK, q_cols), bf16),
+        in_specs=[hbm],
+        out_specs=hbm,
+        scratch_shapes=[pltpu.VMEM((SLOTS, NODE_TOK, q_cols), bf16), dma((OUT_PARTS,)), dma((OUT_PARTS,))],
+        name="hand_over",
+    )(out).reshape(CAP * NODE_TOK, q_cols)
 
 
 def solution(mesh):

time: 134 us -> 116 us (0.87)
  Pallas kernels: 131 us -> 116 us
  local copies, waits for them, and re-layouts: 2.99 us -> 0 us
    pallas_call x1, Pallas kernels: 131 us -> 113 us  [on_device(): pl.pallas_call(functools.partial(fused_kernel, leafs, nodes, width, q_col...]
    unnamed x1 -> x0, local copies, waits for them, and re-layouts: 2.99 us -> none
    pallas_call x0 -> x1, Pallas kernels: none -> 2.37 us  [on_device(): pl.pallas_call(hand_over, out_shape=jax.ShapeDtypeStruct((SLOTS, NODE_TOK...]
where the time goes in v4:
time: 116 us
  Pallas kernels  116 us (100%)
    pallas_call x1, Pallas kernels, on_device(): pl.pallas_call(functools.partial(fused_kernel, leafs, nodes, width, q_col...  113 us
    pallas_call x1, Pallas kernels, on_device(): pl.pallas_call(hand_over, out_shape=jax.ShapeDtypeStruct((SLOTS, NODE_TOK...  2.37 us

profile of v4, /device:TPU:1, one launch (start us, length us, event | category | flops | bytes accessed | tf_op | source)
XLA Modules:
  0.0 115.6 jit_solution(9074472068964907937)
XLA Ops:
  0.0 113.2 %tree_attention.1.from_ref = bf16[31,64,512]{2,1,0:T(8,128)(2,1)} custom-call(s32[16]{0:T(128)} %gen_ref.1, s32[32]{0:T(128)} %part_ref.1, s32[512]{0:T(512)} %parent_ref.1, s32[512,512]{1,0:T(8,128)} %mask_ref.1, bf16[4608]{0:T(1024)(128)(2,1)} %gain_ref.1, f32[1,128]{1,0:T(1,128)} %constant.2.clone.freq_ref, bf16[16,64,1152]{2,1,0:T(8,128)(2,1)} %bitcast.6, ...), custom_call_target="tpu_custom_call" | custom-call | flops 9663676416 | bytes 30000000 | tf_op jit(solution)/shard_map/tree_attention/pallas_call | solution.py:650
  113.2 2.4 %hand_over.1 = bf16[31,64,512]{2,1,0:T(8,128)(2,1)} custom-call(bf16[31,64,512]{2,1,0:T(8,128)(2,1)} %tree_attention.1.from_ref), custom_call_target="tpu_custom_call" | custom-call | tf_op jit(solution)/shard_map/hand_over/pallas_call | solution.py:711

commit v5 on v4

--- a/solution.py
+++ b/solution.py
@@ -37,9 +37,9 @@
     gen_ref, part_ref, parent_ref, mask_ref, gain_ref, freq_ref, tok_ref, wq_ref, wk_ref, wv_ref,
     out_ref,
     held, pieces, weights, scaled, acc, squares, angle_cos, angle_sin, made, send, recv, near, far,
-    query, pool, numer, total, ids_out, ids_in, table_vm, gain_vm,
+    result_vm, query, pool, numer, total, ids_out, ids_in, table_vm, gain_vm,
     depth_sm, index_sm, start_sm, end_sm, table_sm, place_sm,
-    load_sem, own_sem, full_send, full_recv, half_send, half_recv, ids_send, ids_recv, table_sem,
+    out_sem, load_sem, own_sem, full_send, full_recv, half_send, half_recv, ids_send, ids_recv, table_sem,
     slot_send, slot_recv, chip_send, chip_recv, core_send, core_recv,
 ):
     me = lax.axis_index("leaf")
@@ -511,19 +511,31 @@
                 for q in range(CHUNKS):
                     for g in range(groups):
                         start = (q * groups + g) * TOK
-                        out_ref[slots[n], pl.ds(q * TOK, TOK), pl.ds((h * groups + g) * HD, HD)] = results[n, h][
+                        result_vm[slots[n], pl.ds(q * TOK, TOK), pl.ds((h * groups + g) * HD, HD)] = results[n, h][
                             start : start + TOK
                         ]
 
+        def store(i, size):
+            at = pl.ds(i * BATCH, size)
+            return pltpu.make_async_copy(result_vm.at[at], out_ref.at[at], out_sem.at[i])
+
         whole, rest = SLOTS // BATCH, SLOTS % BATCH
 
         def step(i, carry):
             batch([i * BATCH + n for n in range(BATCH)])
+            if final:
+                store(i, BATCH).start()
             return carry
 
         lax.fori_loop(0, whole, step, 0)
         if rest:
             batch(list(range(whole * BATCH, SLOTS)))
+        if final:
+            if rest:
+                store(whole, rest).start()
+                store(whole, rest).wait()
+            for i in range(whole):
+                store(i, BATCH).wait()
 
     def one_chunk(c, carry):
         accumulate(z, c, True)
@@ -568,17 +580,22 @@
             slot_copy(step, c).start()
         recv[c, me] = send[c, me]
 
-        @pl.when(c >= 1)
-        def _():
-            export_start(c - 1)
-
-        @pl.when(c >= 2)
-        def _():
-            export_core(c - 2)
+        def exports():
+            @pl.when(c >= 1)
+            def _():
+                export_start(c - 1)
+
+            @pl.when(c >= 2)
+            def _():
+                export_core(c - 2)
 
         @pl.when(c + 1 < SUBS)
         def _():
-            pass_on(c + 1)
+            pass_on(c + 1, exports)
+
+        @pl.when(c + 1 == SUBS)
+        def _():
+            exports()
 
         return carry
 
@@ -651,7 +668,7 @@
         functools.partial(fused_kernel, leafs, nodes, width, q_cols, k_cols),
         out_shape=jax.ShapeDtypeStruct((SLOTS, NODE_TOK, q_cols), bf16),
         in_specs=[smem, smem, smem, vmem, vmem, vmem, hbm, hbm, hbm, hbm],
-        out_specs=vmem,
+        out_specs=hbm,
         scratch_shapes=[
             pltpu.VMEM((nodes, NODE_TOK, feat), bf16),
             pltpu.VMEM((4, SUBS, nodes // 2, TOK, feat), bf16),
@@ -666,6 +683,7 @@
             pltpu.VMEM((SUBS, leafs, TOK, q_cols), bf16),
             pltpu.VMEM((leafs, TOK, q_cols), bf16),
             pltpu.VMEM((SUBS, leafs, TOK, 2 * k_cols), bf16),
+            pltpu.VMEM((SLOTS, NODE_TOK, q_cols), bf16),
             pltpu.VMEM((CHUNKS, leafs, TOK, q_cols), bf16),
             pltpu.VMEM((CHUNKS, leafs + leafs * EXPORT, TOK, 2 * k_cols), bf16),
             pltpu.VMEM((SLOTS, heads, head_rows, HD), f32),
@@ -680,6 +698,7 @@
             pltpu.SMEM((leafs,), i32),
             pltpu.SMEM((32, 128), i32),
             pltpu.SMEM((SLOTS * ANC,), i32),
+            dma((-(-SLOTS // BATCH),)),
             dma((3,)),
             dma((CHUNKS,)),
             dma((2, 2, SUBS)),

time: 116 us -> 113 us (0.974)
  Pallas kernels: 116 us -> 113 us
    pallas_call x1, Pallas kernels: 113 us -> 111 us  [on_device(): pl.pallas_call(functools.partial(fused_kernel, leafs, nodes, width, q_col...]
where the time goes in v5:
time: 113 us
  Pallas kernels  113 us (100%)
    pallas_call x1, Pallas kernels, on_device(): pl.pallas_call(functools.partial(fused_kernel, leafs, nodes, width, q_col...  111 us
    pallas_call x1, Pallas kernels, on_device(): pl.pallas_call(hand_over, out_shape=jax.ShapeDtypeStruct((SLOTS, NODE_TOK...  2.37 us

profile of v5, /device:TPU:1, one launch (start us, length us, event | category | flops | bytes accessed | tf_op | source)
XLA Modules:
  0.0 113.0 jit_solution(6918052871695199004)
XLA Ops:
  0.0 110.7 %tree_attention.1.from_ref = bf16[31,64,512]{2,1,0:T(8,128)(2,1)} custom-call(s32[16]{0:T(128)} %gen_ref.1, s32[32]{0:T(128)} %part_ref.1, s32[512]{0:T(512)} %parent_ref.1, s32[512,512]{1,0:T(8,128)} %mask_ref.1, bf16[4608]{0:T(1024)(128)(2,1)} %gain_ref.1, f32[1,128]{1,0:T(1,128)} %constant.2.clone.freq_ref, bf16[16,64,1152]{2,1,0:T(8,128)(2,1)} %bitcast.6, ...), custom_call_target="tpu_custom_call" | custom-call | flops 9663676416 | bytes 30000000 | tf_op jit(solution)/shard_map/tree_attention/pallas_call | solution.py:667
  110.7 2.4 %hand_over.1 = bf16[31,64,512]{2,1,0:T(8,128)(2,1)} custom-call(bf16[31,64,512]{2,1,0:T(8,128)(2,1)} %tree_attention.1.from_ref), custom_call_target="tpu_custom_call" | custom-call | tf_op jit(solution)/shard_map/hand_over/pallas_call | solution.py:730

commit v6 on v5

--- a/solution.py
+++ b/solution.py
@@ -19,7 +19,7 @@
 SUBS = 2 * CHUNKS
 SUB = TOK // 2
 SLOTS = CAP
-BATCH = 8
+BATCH = 16
 OUT_PARTS = 8
 CHIP_STEPS = [(2, 2), (0, 1), (1, 0), (0, 3), (3, 0), (2, 1), (1, 2), (2, 3), (3, 2), (0, 2), (2, 0), (1, 1), (3, 3), (1, 3), (3, 1)]
 SLOT_STEPS = [(2, 2, 0), (0, 1, 0), (1, 0, 0), (0, 3, 0), (3, 0, 0), (2, 1, 0), (1, 2, 0), (2, 3, 0), (3, 2, 0), (0, 2, 0), (2, 0, 0), (1, 1, 0), (3, 3, 0), (1, 3, 0), (3, 1, 0), (2, 2, 1), (0, 1, 1), (1, 0, 1), (0, 3, 1), (3, 0, 1), (2, 1, 1), (1, 2, 1), (2, 3, 1), (3, 2, 1), (0, 2, 1), (2, 0, 1), (1, 1, 1), (3, 3, 1), (1, 3, 1), (3, 1, 1), (0, 0, 1)]

time: 113 us -> 113 us (level)
  no operation moved by 1% of the time
where the time goes in v6:
time: 113 us
  Pallas kernels  113 us (100%)
    pallas_call x1, Pallas kernels, on_device(): pl.pallas_call(functools.partial(fused_kernel, leafs, nodes, width, q_col...  110 us
    pallas_call x1, Pallas kernels, on_device(): pl.pallas_call(hand_over, out_shape=jax.ShapeDtypeStruct((SLOTS, NODE_TOK...  2.37 us

profile of v6, /device:TPU:1, one launch (start us, length us, event | category | flops | bytes accessed | tf_op | source)
XLA Modules:
  0.0 112.8 jit_solution(7657475621830429657)
XLA Ops:
  0.0 110.2 %tree_attention.1.from_ref = bf16[31,64,512]{2,1,0:T(8,128)(2,1)} custom-call(s32[16]{0:T(128)} %gen_ref.1, s32[32]{0:T(128)} %part_ref.1, s32[512]{0:T(512)} %parent_ref.1, s32[512,512]{1,0:T(8,128)} %mask_ref.1, bf16[4608]{0:T(1024)(128)(2,1)} %gain_ref.1, f32[1,128]{1,0:T(1,128)} %constant.2.clone.freq_ref, bf16[16,64,1152]{2,1,0:T(8,128)(2,1)} %bitcast.6, ...), custom_call_target="tpu_custom_call" | custom-call | flops 9663676416 | bytes 30000000 | tf_op jit(solution)/shard_map/tree_attention/pallas_call | solution.py:667
  110.2 2.4 %hand_over.1 = bf16[31,64,512]{2,1,0:T(8,128)(2,1)} custom-call(bf16[31,64,512]{2,1,0:T(8,128)(2,1)} %tree_attention.1.from_ref), custom_call_target="tpu_custom_call" | custom-call | tf_op jit(solution)/shard_map/hand_over/pallas_call | solution.py:730
